TPU v7x, 32 devices: a whole 2x2x4 slice. The times are simulated.
32 devices in a mesh: ctx: 8 (over z, x), head: 4 (over y, core).
Axes of the slice: x: 2, y: 2, z: 4, core: 2. Of those that a mesh axis runs over, the one named last changes fastest.
Arguments:
- queries: bfloat16 [512, 64, 128], P('ctx', 'head'), may hold values from -24 to 24
- cache_keys: bfloat16 [2048, 8, 128], P('ctx', 'head'), may hold values from -24 to 24
- cache_values: bfloat16 [2048, 8, 128], P('ctx', 'head'), may hold values from -6 to 6
- new_keys: bfloat16 [512, 8, 128], P('ctx', 'head'), may hold values from -6 to 6
- new_values: bfloat16 [512, 8, 128], P('ctx', 'head'), may hold values from -6 to 6
- frame_of_slot: int32 [8], P('ctx'), may hold values from 0 to 7, each once
- slopes: float32 [64], P('head'), may hold values from 0.002 to 0.1
Outputs:
- attended: bfloat16 [512, 8192], P('ctx')
Inputs may be any that keep to these rules, and one draw needn't show every extreme that they name: `frame_of_slot`: each frame number 0 to 7 stands in exactly one slot.
All inputs are finite; a program needn't handle non-finite values.
Results may differ from a plain program's by a relative error of at most 0.0085.
Values may be sent and summed in bfloat16 or wider, within the bound.
A program may use at most 64 MiB of HBM per device.

v0:
```python
import jax
import jax.numpy as jnp
from jax import lax
from jax.sharding import PartitionSpec as P

FRAME = 256


def from_partner(value, axis, apart):
    return lax.ppermute(value, axis, [(i, i ^ 1 << apart) for i in range(lax.axis_size(axis))])


def update(state, score, values):
    acc, high, total = state
    new_high = jnp.maximum(high, jnp.max(score, axis=-1))
    corr = jnp.exp(high - new_high)
    expo = jnp.exp(score - new_high[..., None])
    total = total * corr + jnp.sum(expo, axis=-1)
    weight = expo.astype(jnp.bfloat16)
    acc = acc * corr[..., None] + jnp.einsum(
        "rgqk,kgd->rgqd", weight, values, preferred_element_type=jnp.float32
    )
    return (acc, new_high, total)


def attend(
    q_rows,
    state,
    cache_keys,
    cache_values,
    key_frames,
    new_keys,
    new_values,
    slopes,
    key_start,
    cache_frames,
):
    rows, local_heads, width = q_rows.shape
    groups = cache_keys.shape[1]
    group = local_heads // groups
    scale = 1.0 / width**0.5
    query = q_rows.reshape(rows, groups, group, width)
    qpos = jnp.arange(rows, dtype=jnp.int32)
    qframe = (cache_frames + qpos // FRAME).astype(jnp.float32)
    slope = slopes.reshape(groups, group)
    frames = key_frames.shape[0]
    kblocks = cache_keys.reshape(frames, FRAME, groups, width)
    vblocks = cache_values.reshape(frames, FRAME, groups, width)

    def scan_step(carry, items):
        kb, vb, fb = items
        score = jnp.einsum("rgqd,kgd->rgqk", query, kb, preferred_element_type=jnp.float32) * scale
        distance = qframe - fb.astype(jnp.float32)
        score = score - slope[None, :, :, None] * distance[:, None, None, None]
        return (update(carry, score, vb), None)

    state, _ = lax.scan(scan_step, state, (kblocks, vblocks, key_frames))
    kpos = key_start + jnp.arange(new_keys.shape[0], dtype=jnp.int32)
    kframe = (cache_frames + kpos // FRAME).astype(jnp.float32)
    score = (
        jnp.einsum("rgqd,kgd->rgqk", query, new_keys, preferred_element_type=jnp.float32) * scale
    )
    score = score - slope[None, :, :, None] * (qframe[:, None] - kframe[None, :])[:, None, None, :]
    visible = kpos[None, :] <= qpos[:, None]
    score = jnp.where(visible[:, None, None, :], score, -1e30)
    return update(state, score, new_values)


def combine_sources(acc, high, total):
    top = jnp.max(high, axis=0)
    scaling = jnp.exp(high - top[None])
    return jnp.sum(acc * scaling[..., None], axis=0) / jnp.sum(total * scaling, axis=0)[..., None]


def on_device(queries, cache_keys, cache_values, new_keys, new_values, frame_of_slot, slopes):
    rows, local_heads, width = queries.shape
    groups = cache_keys.shape[1]
    group = local_heads // groups
    shards = lax.axis_size("ctx")
    position = lax.axis_index("ctx")
    cache_frames = frame_of_slot.shape[0] * shards
    parity = position % 2
    other = 1 - parity
    keep_keys = lax.dynamic_slice_in_dim(cache_keys, parity, 1, 1)
    keep_values = lax.dynamic_slice_in_dim(cache_values, parity, 1, 1)
    keep_new_keys = lax.dynamic_slice_in_dim(new_keys, parity, 1, 1)
    keep_new_values = lax.dynamic_slice_in_dim(new_values, parity, 1, 1)
    sent = (
        lax.dynamic_slice_in_dim(cache_keys, other, 1, 1),
        lax.dynamic_slice_in_dim(cache_values, other, 1, 1),
        lax.dynamic_slice_in_dim(new_keys, other, 1, 1),
        lax.dynamic_slice_in_dim(new_values, other, 1, 1),
    )
    got_keys, got_values, got_new_keys, got_new_values = from_partner(
        (sent[0], sent[1], sent[2], sent[3]), "ctx", 0
    )
    got_frames = from_partner(frame_of_slot, "ctx", 0)
    pair_keys = jnp.concatenate([keep_keys, got_keys], axis=0)
    pair_values = jnp.concatenate([keep_values, got_values], axis=0)
    pair_frames = jnp.concatenate([frame_of_slot, got_frames], axis=0)
    lower = parity == 0
    pair_new_keys = jnp.where(
        lower,
        jnp.concatenate([keep_new_keys, got_new_keys], axis=0),
        jnp.concatenate([got_new_keys, keep_new_keys], axis=0),
    )
    pair_new_values = jnp.where(
        lower,
        jnp.concatenate([keep_new_values, got_new_values], axis=0),
        jnp.concatenate([got_new_values, keep_new_values], axis=0),
    )
    pair_start = (position - parity) * new_keys.shape[0]
    split_heads = jnp.transpose(queries.reshape(rows, groups, group, width), (1, 0, 2, 3))
    outgoing = jnp.tile(split_heads, (shards // groups, 1, 1, 1))
    everyone = lax.all_to_all(outgoing, "ctx", split_axis=0, concat_axis=0, tiled=True).reshape(
        shards * rows, group, width
    )
    my_slopes = lax.dynamic_slice_in_dim(slopes, parity * group, group)
    count = rows * shards
    acc, high, total = attend(
        everyone,
        (
            jnp.zeros((count, 1, group, width), jnp.float32),
            jnp.full((count, 1, group), -1e30, jnp.float32),
            jnp.zeros((count, 1, group), jnp.float32),
        ),
        pair_keys,
        pair_values,
        pair_frames,
        pair_new_keys,
        pair_new_values,
        my_slopes,
        pair_start,
        cache_frames,
    )
    acc, high, total = (
        lax.all_to_all(acc, "ctx", split_axis=0, concat_axis=0, tiled=True),
        lax.all_to_all(high, "ctx", split_axis=0, concat_axis=0, tiled=True),
        lax.all_to_all(total, "ctx", split_axis=0, concat_axis=0, tiled=True),
    )
    acc = acc.reshape(shards // groups, groups, rows, group, width)
    high = high.reshape(shards // groups, groups, rows, group)
    total = total.reshape(shards // groups, groups, rows, group)
    merged = jnp.transpose(combine_sources(acc, high, total), (1, 0, 2, 3))
    result = merged.astype(jnp.bfloat16).reshape(rows, local_heads * width)
    return lax.all_gather(result, "head", axis=1, tiled=True)


def solution(mesh):
    return jax.shard_map(
        on_device,
        mesh=mesh,
        in_specs=(
            P("ctx", "head", None),
            P("ctx", "head", None),
            P("ctx", "head", None),
            P("ctx", "head", None),
            P("ctx", "head", None),
            P("ctx"),
            P("head"),
        ),
        out_specs=P("ctx", None),
        check_vma=False,
    )
```

profile of v0, /device:TPU:0, one launch (start us, length us, event | category | flops | bytes accessed | tf_op | source)
XLA Modules:
  0.0 169.1 jit_solution(3091976381370423439)
XLA Ops:
  6.5 1.1 copy.82
  7.6 1.2 tile.4
  8.8 7.4 %all-to-all-start = ((bf16[8,64,8,128]{3,1,2,0:T(8,128)(2,1)}), bf16[8,64,8,128]{3,1,2,0:T(8,128)(2,1)S(1)}, u32[]{:S(2)}, u32[]{:S(2)}) async-start(bf16[8,64,8,128]{3,1,2,0:T(8,128)(2,1)} %bitcast.4), calls=%async_computation | async-start | bytes 2097152 | tf_op jit(solution)/shard_map/all_to_all | solution.py:115
  16.2 0.5 constant_dynamic-slice_fusion.5
  16.8 0.6 copy.109
  17.4 2.0 %collective-permute-start = (bf16[256,1,128]{2,0,1:T(8,128)(2,1)}, bf16[256,1,128]{2,0,1:T(8,128)(2,1)}, u32[]{:S(2)}, u32[]{:S(2)}) collective-permute-start(bf16[256,1,128]{2,0,1:T(8,128)(2,1)} %copy.109), channel_id=1, source_target_pairs={{0,4},{4,0},{8,12},{12,8},{16,20},{20,16},{24,28},{28,24},{1,5},{5... | collective-permute-start | bytes 196616 | tf_op jit(solution)/shard_map/ppermute | solution.py:10
  19.4 0.6 copy.111
  20.1 2.0 %collective-permute-start.1 = (s32[1]{0:T(128)}, s32[1]{0:T(128)}, u32[]{:S(2)}, u32[]{:S(2)}) collective-permute-start(s32[1]{0:T(128)} %param.14), channel_id=1, source_target_pairs={{0,4},{4,0},{8,12},{12,8},{16,20},{20,16},{24,28},{28,24},{1,5},{5... | collective-permute-start | bytes 20 | tf_op jit(solution)/shard_map/ppermute | solution.py:10
  22.1 0.7 constant_dynamic-slice_fusion.1
  23.6 0.6 copy.108
  24.2 1.4 copy.122
  25.6 0.6 dynamic_slice.40
  26.1 0.7 iota_compare_fusion
  26.9 0.8 broadcast_subtract_fusion
  27.6 2.2 %collective-permute-done.1 = s32[1]{0:T(128)} collective-permute-done((s32[1]{0:T(128)}, s32[1]{0:T(128)}, u32[]{:S(2)}, u32[]{:S(2)}) %collective-permute-start.1) | collective-permute-done | bytes 36 | tf_op jit(solution)/shard_map/ppermute | solution.py:10
  29.8 1.3 pad_add_fusion
  31.2 0.9 pad_maximum_fusion
  32.1 0.9 pad_maximum_fusion.1
  32.9 9.1 %all-to-all-done = bf16[8,64,8,128]{3,1,2,0:T(8,128)(2,1)S(1)} async-done(((bf16[8,64,8,128]{3,1,2,0:T(8,128)(2,1)}), bf16[8,64,8,128]{3,1,2,0:T(8,128)(2,1)S(1)}, u32[]{:S(2)}, u32[]{:S(2)}) %all-to-all-start) | async-done | bytes 1048608 | tf_op jit(solution)/shard_map/all_to_all | solution.py:115
  42.0 0.7 copy.83
  42.7 0.3 copy-done.1
  43.0 0.1 copy.87
  43.1 20.0 %while.15 = (s32[]{:T(128)}, f32[512,1,8,128]{0,3,2,1:T(8,128)S(1)}, f32[512,1,8]{0,2,1:T(8,128)S(1)}, f32[512,1,8]{0,2,1:T(8,128)S(1)}, bf16[2,256,1,128]{3,1,2...) while((s32[]{:T(128)}, ...), condition=%wide.region_3.4_spmd.clone, body=%wide.region_0.3_spmd.clone.sunk | while | flops 550012416 | bytes 35066064 | solution.py:57
  43.1 1.2 dynamic_slice.73
  44.9 0.6 broadcast_multiply_fusion.2
  45.6 2.6 %bitcast_reduce_fusion.2 = (f32[512,8]{0,1:T(8,128)S(1)}, f32[256,512,8]{1,0,2:T(8,128)}) fusion(f32[512,8]{0,1:T(8,128)S(1)} %broadcast_multiply_fusion.2, bf16[512,1,8,128]{3,0,2,1:T(8,128)(2,1)S(1)} %get-tuple-element.262, bf16[2,256,1,128]{3,1,2,0:T(8,128)(2,1)S(1)} %get-tuple-element.261, s32[]{:T(128)} %get-tuple-element.246), kind=kOutput, calls=%fused_computation.2.clone.1 | convolution fusion | flops 271577088 | bytes 5341188 | tf_op jit(solution)/shard_map/while/body/eval_jaxpr/rgqd,kgd->rgqk/dot_general | solution.py:52
  48.2 3.2 %fusion.76 = f32[512,8]{0,1:T(8,128)S(1)} fusion(f32[256,512,8]{1,0,2:T(8,128)} %get-tuple-element.231, f32[512,8]{0,1:T(8,128)S(1)} %bitcast.160, f32[512,8]{0,1:T(8,128)S(1)} %broadcast_multiply_fusion.2), kind=kLoop, calls=%fused_computation.5.clone.1 | loop fusion | flops 4190208 | bytes 4243456 | tf_op jit(solution)/shard_map/while/body/eval_jaxpr/reduce_sum | solution.py:18
  51.5 0.2 copy-done
  51.7 1.4 bitcast_add_fusion.6
  53.1 1.2 dynamic_slice.73
  55.0 0.6 broadcast_multiply_fusion.2
  55.6 2.6 %bitcast_reduce_fusion.2 = (f32[512,8]{0,1:T(8,128)S(1)}, f32[256,512,8]{1,0,2:T(8,128)}) fusion(f32[512,8]{0,1:T(8,128)S(1)} %broadcast_multiply_fusion.2, bf16[512,1,8,128]{3,0,2,1:T(8,128)(2,1)S(1)} %get-tuple-element.262, bf16[2,256,1,128]{3,1,2,0:T(8,128)(2,1)S(1)} %get-tuple-element.261, s32[]{:T(128)} %get-tuple-element.246), kind=kOutput, calls=%fused_computation.2.clone.1 | convolution fusion | flops 271577088 | bytes 5341188 | tf_op jit(solution)/shard_map/while/body/eval_jaxpr/rgqd,kgd->rgqk/dot_general | solution.py:52
  58.3 3.2 %fusion.76 = f32[512,8]{0,1:T(8,128)S(1)} fusion(f32[256,512,8]{1,0,2:T(8,128)} %get-tuple-element.231, f32[512,8]{0,1:T(8,128)S(1)} %bitcast.160, f32[512,8]{0,1:T(8,128)S(1)} %broadcast_multiply_fusion.2), kind=kLoop, calls=%fused_computation.5.clone.1 | loop fusion | flops 4190208 | bytes 4243456 | tf_op jit(solution)/shard_map/while/body/eval_jaxpr/reduce_sum | solution.py:18
  61.5 0.2 copy-done
  61.7 1.4 bitcast_add_fusion.6
  63.2 1.4 copy.91
  64.6 1.5 fusion.65
  66.1 1.3 copy-done.2
  67.4 0.3 fusion.30
  67.7 0.5 broadcast.249
  68.3 0.6 reduce.4
  68.9 0.1 copy.123
  69.0 0.8 reshape.276
  69.8 3.6 %all-to-all-start.3 = ((f32[8,1,512]{2,1,0:T(1,128)}), f32[8,1,512]{2,1,0:T(1,128)S(1)}, u32[]{:S(2)}, u32[]{:S(2)}) async-start(f32[8,1,512]{2,1,0:T(1,128)} %reshape.276), calls=%async_computation.3 | async-start | bytes 32768 | tf_op jit(solution)/shard_map/all_to_all | solution.py:139
  73.4 2.1 %collective-permute-start.4 = (bf16[64,1,128]{2,0,1:T(8,128)(2,1)S(1)}, bf16[64,1,128]{2,0,1:T(8,128)(2,1)S(1)}, u32[]{:S(2)}, u32[]{:S(2)}) collective-permute-start(bf16[64,1,128]{2,0,1:T(8,128)(2,1)S(1)} %copy.115), channel_id=1, source_target_pairs={{0,4},{4,0},{8,12},{12,8},{16,20},{20,16},{24,28},{28,24},{1,5},{5... | collective-permute-start | bytes 49160 | tf_op jit(solution)/shard_map/ppermute | solution.py:10
  75.5 0.6 reduce.6
  76.1 0.1 copy.124
  76.2 0.8 reshape.274
  77.0 2.9 %all-to-all-done.3 = f32[8,1,512]{2,1,0:T(1,128)S(1)} async-done(((f32[8,1,512]{2,1,0:T(1,128)}), f32[8,1,512]{2,1,0:T(1,128)S(1)}, u32[]{:S(2)}, u32[]{:S(2)}) %all-to-all-start.3) | async-done | bytes 16416 | tf_op jit(solution)/shard_map/all_to_all | solution.py:139
  80.0 3.3 %all-to-all-start.2 = ((f32[8,1,512]{2,1,0:T(1,128)}), f32[8,1,512]{2,1,0:T(1,128)S(1)}, u32[]{:S(2)}, u32[]{:S(2)}) async-start(f32[8,1,512]{2,1,0:T(1,128)} %reshape.274), calls=%async_computation.2 | async-start | bytes 32768 | tf_op jit(solution)/shard_map/all_to_all | solution.py:138
  83.3 3.4 %bitcast_add_fusion.2 = f32[512,1,8,128]{0,3,2,1:T(8,128)} fusion(f32[512,1,8,128]{0,3,2,1:T(8,128)S(1)} %get-tuple-element.59, f32[512,8]{0,1:T(8,128)S(1)} %get-tuple-element.152, f32[512,1,8,128]{0,3,2,1:T(8,128)} %copy-done.2, f32[512,8]{0,1:T(8,128)S(1)} %bitcast.173, bf16[64,128]{1,0:T(8,128)(2,1)S(1)} %bitcast.177, ...), kind=kOutput, calls=%fused_computation.39 | convolution fusion | flops 136462336 | bytes 6356993 | tf_op jit(solution)/shard_map/rgqk,kgd->rgqd/dot_general | solution.py:20
  86.7 2.9 %copy.96 = f32[512,1,8,128]{3,2,1,0:T(8,128)} copy(f32[512,1,8,128]{0,3,2,1:T(8,128)} %bitcast_add_fusion.2) | data formatting | bytes 4194304 | tf_op jit(solution)/shard_map/add | solution.py:20
  89.7 0.1 all-to-all-done.2
  89.8 5.8 %all-to-all-start.1 = ((f32[512,1,8,128]{3,2,1,0:T(8,128)}), f32[512,1,8,128]{3,2,1,0:T(8,128)S(1)}, u32[]{:S(2)}, u32[]{:S(2)}) async-start(f32[512,1,8,128]{3,2,1,0:T(8,128)} %copy.96), calls=%async_computation.1 | async-start | bytes 4194304 | tf_op jit(solution)/shard_map/all_to_all | solution.py:137
  95.6 0.7 reduce.5
  96.3 0.5 reshape.277
  96.8 0.7 reduce.7
  97.4 0.5 reshape.275
  98.0 44.4 %all-to-all-done.1 = f32[512,1,8,128]{3,2,1,0:T(8,128)S(1)} async-done(((f32[512,1,8,128]{3,2,1,0:T(8,128)}), f32[512,1,8,128]{3,2,1,0:T(8,128)S(1)}, u32[]{:S(2)}, u32[]{:S(2)}) %all-to-all-start.1) | async-done | bytes 2097184 | tf_op jit(solution)/shard_map/all_to_all | solution.py:137
  142.4 0.7 multiply_reduce_fusion
  143.1 0.2 fusion.36
  143.4 0.8 copy.120
  144.2 15.9 %all-gather.2.cloned.1.call-done = bf16[64,8192]{1,0:T(8,128)(2,1)} async-done(((bf16[64,2048]{1,0:T(8,128)(2,1)}), bf16[64,8192]{1,0:T(8,128)(2,1)}) %all-gather.2.cloned.1.call-update) | async-done | bytes 1048592 | tf_op jit(solution)/shard_map/all_gather | solution.py:146
  160.0 2.3 %copy.139 = bf16[64,8192]{1,0:T(8,128)(2,1)} copy(bf16[64,8192]{1,0:T(8,128)(2,1)} %all-gather.2.cloned.1.call-done) | data formatting | bytes 2097152
  (54 shorter events, 0.4 us)
Async XLA Ops:
  6.5 9.7 %copy-start.4 = (bf16[256,2,128]{2,1,0:T(2,128)(2,1)S(1)}, bf16[256,2,128]{2,1,0:T(2,128)(2,1)}, u32[]{:S(2)}) copy-start(bf16[256,2,128]{2,1,0:T(2,128)(2,1)} %param.10) | copy-start | bytes 393220
  6.5 9.7 %copy-start.3 = (bf16[256,2,128]{2,1,0:T(2,128)(2,1)S(1)}, bf16[256,2,128]{2,1,0:T(2,128)(2,1)}, u32[]{:S(2)}) copy-start(bf16[256,2,128]{2,1,0:T(2,128)(2,1)} %param.11) | copy-start | bytes 393220
  8.8 13.3 %copy-start.6 = (bf16[64,2,128]{2,1,0:T(2,128)(2,1)S(1)}, bf16[64,2,128]{2,1,0:T(2,128)(2,1)}, u32[]{:S(2)}) copy-start(bf16[64,2,128]{2,1,0:T(2,128)(2,1)} %param.13) | copy-start | bytes 98308
  8.8 13.3 %copy-start.7 = (bf16[64,2,128]{2,1,0:T(2,128)(2,1)S(1)}, bf16[64,2,128]{2,1,0:T(2,128)(2,1)}, u32[]{:S(2)}) copy-start(bf16[64,2,128]{2,1,0:T(2,128)(2,1)} %param.12) | copy-start | bytes 98308
  8.8 16.7 %copy-start.12 = (f32[16]{0:T(128)S(1)}, f32[16]{0:T(128)}, u32[]{:S(2)}) copy-start(f32[16]{0:T(128)} %param.15) | copy-start | bytes 196
  8.8 33.2 %all-to-all-start = ((bf16[8,64,8,128]{3,1,2,0:T(8,128)(2,1)}), bf16[8,64,8,128]{3,1,2,0:T(8,128)(2,1)S(1)}, u32[]{:S(2)}, u32[]{:S(2)}) async-start(bf16[8,64,8,128]{3,1,2,0:T(8,128)(2,1)} %bitcast.4), calls=%async_computation | async-start | bytes 2097152 | tf_op jit(solution)/shard_map/all_to_all | solution.py:115
  17.4 13.7 %collective-permute-start = (bf16[256,1,128]{2,0,1:T(8,128)(2,1)}, bf16[256,1,128]{2,0,1:T(8,128)(2,1)}, u32[]{:S(2)}, u32[]{:S(2)}) collective-permute-start(bf16[256,1,128]{2,0,1:T(8,128)(2,1)} %copy.109), channel_id=1, source_target_pairs={{0,4},{4,0},{8,12},{12,8},{16,20},{20,16},{24,28},{28,24},{1,5},{5... | collective-permute-start | bytes 196616 | tf_op jit(solution)/shard_map/ppermute | solution.py:10
  20.1 12.0 %collective-permute-start.2 = (bf16[256,1,128]{2,0,1:T(8,128)(2,1)}, bf16[256,1,128]{2,0,1:T(8,128)(2,1)}, u32[]{:S(2)}, u32[]{:S(2)}) collective-permute-start(bf16[256,1,128]{2,0,1:T(8,128)(2,1)} %copy.111), channel_id=1, source_target_pairs={{0,4},{4,0},{8,12},{12,8},{16,20},{20,16},{24,28},{28,24},{1,5},{5... | collective-permute-start | bytes 196616 | tf_op jit(solution)/shard_map/ppermute | solution.py:10
  20.1 9.8 %collective-permute-start.1 = (s32[1]{0:T(128)}, s32[1]{0:T(128)}, u32[]{:S(2)}, u32[]{:S(2)}) collective-permute-start(s32[1]{0:T(128)} %param.14), channel_id=1, source_target_pairs={{0,4},{4,0},{8,12},{12,8},{16,20},{20,16},{24,28},{28,24},{1,5},{5... | collective-permute-start | bytes 20 | tf_op jit(solution)/shard_map/ppermute | solution.py:10
  22.9 41.7 %collective-permute-start.3 = (bf16[64,1,128]{2,0,1:T(8,128)(2,1)S(1)}, bf16[64,1,128]{2,0,1:T(8,128)(2,1)}, u32[]{:S(2)}, u32[]{:S(2)}) collective-permute-start(bf16[64,1,128]{2,0,1:T(8,128)(2,1)S(1)} %copy.113), channel_id=1, source_target_pairs={{0,4},{4,0},{8,12},{12,8},{16,20},{20,16},{24,28},{28,24},{1,5},{5... | collective-permute-start | bytes 49160 | tf_op jit(solution)/shard_map/ppermute | solution.py:10
  42.0 1.0 copy-start.1
  48.2 3.5 %copy-start = (f32[256,512,8]{1,0,2:T(8,128)S(1)}, f32[256,512,8]{1,0,2:T(8,128)}, u32[]{:S(2)}) copy-start(f32[256,512,8]{1,0,2:T(8,128)} %get-tuple-element.231) | copy-start | bytes 12582916 | tf_op jit(solution)/shard_map/while
  58.3 3.5 %copy-start = (f32[256,512,8]{1,0,2:T(8,128)S(1)}, f32[256,512,8]{1,0,2:T(8,128)}, u32[]{:S(2)}) copy-start(f32[256,512,8]{1,0,2:T(8,128)} %get-tuple-element.231) | copy-start | bytes 12582916 | tf_op jit(solution)/shard_map/while
  63.2 1.4 copy-start.5
  63.2 1.4 copy-start.10
  63.2 1.4 copy-start.11
  66.1 1.3 copy-start.2
  66.1 7.3 %copy-start.9 = (bf16[64,1,128]{2,1,0:T(2,128)(2,1)S(1)}, bf16[64,1,128]{2,1,0:T(2,128)(2,1)}, u32[]{:S(2)}) copy-start(bf16[64,1,128]{2,1,0:T(2,128)(2,1)} %get-tuple-element.161) | copy-start | bytes 49156
  66.1 9.4 %copy-start.8 = (bf16[64,1,128]{2,1,0:T(2,128)(2,1)S(1)}, bf16[64,1,128]{2,1,0:T(2,128)(2,1)}, u32[]{:S(2)}) copy-start(bf16[64,1,128]{2,1,0:T(2,128)(2,1)} %get-tuple-element.160) | copy-start | bytes 49156
  69.8 10.2 %all-to-all-start.3 = ((f32[8,1,512]{2,1,0:T(1,128)}), f32[8,1,512]{2,1,0:T(1,128)S(1)}, u32[]{:S(2)}, u32[]{:S(2)}) async-start(f32[8,1,512]{2,1,0:T(1,128)} %reshape.276), calls=%async_computation.3 | async-start | bytes 32768 | tf_op jit(solution)/shard_map/all_to_all | solution.py:139
  73.4 9.9 %collective-permute-start.4 = (bf16[64,1,128]{2,0,1:T(8,128)(2,1)S(1)}, bf16[64,1,128]{2,0,1:T(8,128)(2,1)S(1)}, u32[]{:S(2)}, u32[]{:S(2)}) collective-permute-start(bf16[64,1,128]{2,0,1:T(8,128)(2,1)S(1)} %copy.115), channel_id=1, source_target_pairs={{0,4},{4,0},{8,12},{12,8},{16,20},{20,16},{24,28},{28,24},{1,5},{5... | collective-permute-start | bytes 49160 | tf_op jit(solution)/shard_map/ppermute | solution.py:10
  80.0 9.8 %all-to-all-start.2 = ((f32[8,1,512]{2,1,0:T(1,128)}), f32[8,1,512]{2,1,0:T(1,128)S(1)}, u32[]{:S(2)}, u32[]{:S(2)}) async-start(f32[8,1,512]{2,1,0:T(1,128)} %reshape.274), calls=%async_computation.2 | async-start | bytes 32768 | tf_op jit(solution)/shard_map/all_to_all | solution.py:138
  89.8 52.6 %all-to-all-start.1 = ((f32[512,1,8,128]{3,2,1,0:T(8,128)}), f32[512,1,8,128]{3,2,1,0:T(8,128)S(1)}, u32[]{:S(2)}, u32[]{:S(2)}) async-start(f32[512,1,8,128]{3,2,1,0:T(8,128)} %copy.96), calls=%async_computation.1 | async-start | bytes 4194304 | tf_op jit(solution)/shard_map/all_to_all | solution.py:137
  95.6 64.4 %all-gather.2.cloned.1.call-start = ((), (), s32[]{:S(2)}) async-start(), calls=%async_computation.4 | async-start | bytes 1310720 | tf_op jit(solution)/shard_map/all_gather | solution.py:146
Sparse Core Ops, SparseCore 0:
  144.3 15.7 all-gather.1
where the time goes:
time: 170 us; the launch traced here: 169 us
  waiting for transfers between devices  74.6 us (44%)
  starting transfers between devices  26.3 us (15%)
  local copies, waits for them, and re-layouts  23.4 us (14%)
  other arithmetic  16.2 us (10%)
  between operations  14.4 us (8%)
  matrix products  13 us (8%)
    all_to_all x1, waiting for transfers between devices, on_device(): lax.all_to_all(acc, 'ctx', split_axis=0, concat_axis=0, tiled=True)  44.4 us
    all_gather x1, waiting for transfers between devices, on_device(): return lax.all_gather(result, 'head', axis=1, tiled=True)  15.9 us
    unnamed x41, local copies, waits for them, and re-layouts  10.8 us
    all_to_all x1, waiting for transfers between devices, on_device(): lax.all_to_all(outgoing, 'ctx', split_axis=0, concat_axis=0, tiled=True)  9.08 us
    all_to_all x1, starting transfers between devices, on_device(): lax.all_to_all(outgoing, 'ctx', split_axis=0, concat_axis=0, tiled=True)  7.38 us
    reduce_sum x3, other arithmetic, update(): total = total * corr + jnp.sum(expo, axis=-1)  6.69 us
    dot_general x3, matrix products, update(): jnp.einsum('rgqk,kgd->rgqd', weight, values, preferred_element_type=jnp.f...  6.25 us
    ppermute x5, starting transfers between devices, from_partner(): lax.ppermute(value, axis, [(i, i ^ 1 << apart) for i in range(lax.axis_si...  6.15 us
  transfers between devices with their start and end apart: 10, of which 6 were waited for; matrix products, arithmetic and copies ran while one was open for 24% of the time, Pallas kernels for 0%

commit v1 on v0

--- a/solution.py
+++ b/solution.py
@@ -1,9 +1,426 @@
+import functools
+import math
+
 import jax
 import jax.numpy as jnp
 from jax import lax
+from jax.experimental import pallas as pl
+from jax.experimental.pallas import tpu as pltpu
 from jax.sharding import PartitionSpec as P
 
 FRAME = 256
+MESH = pl.DeviceIdType.MESH
+LOG2E = 1.0 / math.log(2.0)
+PARTS = 2
+
+
+def nt(a, b):
+    return lax.dot_general(a, b, (((1,), (1,)), ((), ())), preferred_element_type=jnp.float32)
+
+
+def tn(a, b):
+    return lax.dot_general(a, b, (((0,), (0,)), ((), ())), preferred_element_type=jnp.float32)
+
+
+def iota(shape, dim):
+    return lax.broadcasted_iota(jnp.int32, shape, dim)
+
+
+def kernel(
+    sizes,
+    q_ref,
+    ck_ref,
+    cv_ref,
+    nk_ref,
+    nv_ref,
+    frame_ref,
+    slope_ref,
+    o_ref,
+    kv,
+    newkv,
+    qb,
+    acc,
+    high,
+    total,
+    part_out,
+    part_in,
+    kv_up,
+    kv_down,
+    kv_recv,
+    q_send,
+    q_recv,
+    p_send,
+    p_recv,
+    o_send,
+    o_recv,
+):
+    cached, fresh, groups, group, width, shards, heads = sizes
+    column = shards // 2
+    rows = group * fresh
+    cache_frames = shards
+    position = lax.axis_index("ctx")
+    me = lax.axis_index("head")
+    side = position % 2
+    place = position // 2
+    across = position + 1 - 2 * side
+    sibling = me + 1 - 2 * (me % 2)
+    peers = [lax.rem(me + 2 * k, heads) for k in range(1, heads // 2)]
+    last = column - 1
+    has_up = place < last
+    has_down = place > 0
+    scale = LOG2E / width**0.5
+    v_at = cached + fresh
+    f_at = 2 * v_at
+
+    barrier = pltpu.get_barrier_semaphore()
+    pl.semaphore_signal(barrier, inc=1, device_id={"ctx": across}, device_id_type=MESH)
+    for other in [sibling] + peers:
+        pl.semaphore_signal(barrier, inc=1, device_id={"head": other}, device_id_type=MESH)
+
+    @pl.when(has_up)
+    def _():
+        pl.semaphore_signal(barrier, inc=1, device_id={"ctx": position + 2}, device_id_type=MESH)
+
+    @pl.when(has_down)
+    def _():
+        pl.semaphore_signal(barrier, inc=1, device_id={"ctx": position - 2}, device_id_type=MESH)
+
+    frame = frame_ref[0].astype(jnp.float32)
+    for g in range(groups):
+        pick = (iota((cached, groups * cached), 1) == groups * iota((cached, groups * cached), 0) + g)
+        pick = pick.astype(jnp.float32).astype(jnp.bfloat16)
+        few = pick[:fresh, : groups * fresh]
+        for src, at, sel, n in (
+            (ck_ref, 0, pick, cached),
+            (nk_ref, cached, few, fresh),
+            (cv_ref, v_at, pick, cached),
+            (nv_ref, v_at + cached, few, fresh),
+        ):
+            kv[place, g, at : at + n, :] = jnp.dot(
+                sel, src[...], preferred_element_type=jnp.float32
+            ).astype(jnp.bfloat16)
+        kv[place, g, f_at : f_at + 16, :] = jnp.full((16, width), frame, jnp.float32).astype(
+            jnp.bfloat16
+        )
+
+    pl.semaphore_wait(
+        barrier, 1 + heads // 2 + jnp.minimum(place, 1) + jnp.minimum(last - place, 1)
+    )
+
+    def up(src, g):
+        return pltpu.make_async_remote_copy(
+            src_ref=kv.at[src, g],
+            dst_ref=kv.at[src, g],
+            send_sem=kv_up.at[src, g],
+            recv_sem=kv_recv.at[src, g],
+            device_id={"ctx": position + 2},
+            device_id_type=MESH,
+        )
+
+    def down(src, g):
+        return pltpu.make_async_remote_copy(
+            src_ref=kv.at[src, g],
+            dst_ref=kv.at[src, g],
+            send_sem=kv_down.at[src, g],
+            recv_sem=kv_recv.at[src, g],
+            device_id={"ctx": position - 2},
+            device_id_type=MESH,
+        )
+
+    for g in range(groups):
+
+        @pl.when(has_up)
+        def _():
+            up(place, g).start()
+
+        @pl.when(has_down)
+        def _():
+            down(place, g).start()
+
+    def q_copy(g):
+        return pltpu.make_async_remote_copy(
+            src_ref=qb.at[0, g],
+            dst_ref=qb.at[1, g],
+            send_sem=q_send.at[g],
+            recv_sem=q_recv.at[g],
+            device_id={"ctx": across},
+            device_id_type=MESH,
+        )
+
+    local = groups * group
+    for g in range(groups):
+        r = iota((rows, local * fresh), 0)
+        want = (r % fresh) * local + r // fresh + g * group
+        pick = (iota((rows, local * fresh), 1) == want).astype(jnp.float32).astype(jnp.bfloat16)
+        qb[0, g] = jnp.dot(pick, q_ref[...], preferred_element_type=jnp.float32).astype(jnp.bfloat16)
+        q_copy(g).start()
+
+    lane = iota((1, rows), 1)
+    token = lane % fresh
+
+    def slope_row(g):
+        head = lane // fresh
+        row = jnp.zeros((1, rows), jnp.float32)
+        for j in range(group):
+            row = jnp.where(head == j, slope_ref[g * group + j], row)
+        return row * LOG2E
+
+    def query_position(r):
+        owner = position if r == 0 else across
+        return owner * fresh + token
+
+    def query_frame(r):
+        return (cache_frames + query_position(r) // FRAME).astype(jnp.float32)
+
+    for i in range(2 * groups):
+        acc[i] = jnp.zeros((width, rows), jnp.float32)
+        high[i] = jnp.full((1, rows), -1e30, jnp.float32)
+        total[i] = jnp.zeros((1, rows), jnp.float32)
+
+    def update(i, score, shift, values):
+        before = high[i]
+        now = jnp.maximum(before, jnp.max(score, axis=0, keepdims=True) + shift)
+        corr = jnp.exp2(before - now)
+        expo = jnp.exp2(score + (shift - now))
+        high[i] = now
+        total[i] = total[i] * corr + jnp.sum(expo, axis=0, keepdims=True)
+        acc[i] = acc[i] * corr + tn(values, expo.astype(jnp.bfloat16))
+
+    def slopes_of(g):
+        if isinstance(g, int):
+            return slope_row(g)
+        row = slope_row(0)
+        for k in range(1, groups):
+            row = jnp.where(g == k, slope_row(k), row)
+        return row
+
+    def attend(src, g):
+        keys = kv[src, g, 0:cached, :]
+        values = kv[src, g, v_at : v_at + cached, :]
+        key_frame = kv[src, g, f_at : f_at + 16, :].astype(jnp.float32)[0:1, 0:1]
+        slope = slopes_of(g)
+        for r in (1, 0):
+            score = nt(keys, qb[r, g]) * scale
+            update(2 * g + r, score, -slope * (query_frame(r) - key_frame), values)
+
+    def attend_new(g):
+        for src in range(column):
+            newkv[0, src * fresh : (src + 1) * fresh, :] = kv[src, g, cached : cached + fresh, :]
+            newkv[1, src * fresh : (src + 1) * fresh, :] = kv[
+                src, g, v_at + cached : v_at + cached + fresh, :
+            ]
+        index = iota((column * fresh, 1), 0)
+        key_position = ((index // fresh) * 2 + side) * fresh + index % fresh
+        key_frame = (cache_frames + key_position // FRAME).astype(jnp.float32)
+        slope = slope_row(g)
+        for r in (1, 0):
+            score = nt(newkv[0], qb[r, g]) * scale - slope * (query_frame(r) - key_frame)
+            score = jnp.where(key_position <= query_position(r), score, -1e30)
+            update(2 * g + r, score, jnp.zeros((1, rows), jnp.float32), newkv[1])
+
+    def step(apart, g, first):
+        low = place - apart
+        top = place + apart
+
+        @pl.when(low >= 0)
+        def _():
+            up(low, g).wait_recv()
+
+            @pl.when(has_up)
+            def _():
+                up(low, g).start()
+
+        @pl.when(top <= last)
+        def _():
+            down(top, g).wait_recv()
+
+            @pl.when(has_down)
+            def _():
+                down(top, g).start()
+
+        @pl.when(first)
+        def _():
+            q_copy(g).wait_recv()
+            attend(place, g)
+
+        @pl.when(low >= 0)
+        def _():
+            attend(low, g)
+
+        @pl.when(top <= last)
+        def _():
+            attend(top, g)
+
+    part_rows = rows // PARTS
+    part_heads = group // PARTS
+
+    def p_copy(i):
+        return pltpu.make_async_remote_copy(
+            src_ref=part_out.at[i],
+            dst_ref=part_in.at[i],
+            send_sem=p_send.at[i],
+            recv_sem=p_recv.at[i],
+            device_id={"ctx": across},
+            device_id_type=MESH,
+        )
+
+    def finish(g):
+        attend_new(g)
+        sub = iota((16, part_rows), 0)
+        for c in range(PARTS):
+            i = g * PARTS + c
+            cols = slice(c * part_rows, (c + 1) * part_rows)
+            sums = total[2 * g + 1, :, cols]
+            part_out[i, 0:width, :] = (acc[2 * g + 1, :, cols] / sums).astype(jnp.bfloat16)
+            lse = high[2 * g + 1, :, cols] + jnp.log(sums) * LOG2E
+            one = lse.astype(jnp.bfloat16).astype(jnp.float32)
+            two = (lse - one).astype(jnp.bfloat16).astype(jnp.float32)
+            three = lse - one - two
+            stats = jnp.where(sub == 0, one, jnp.where(sub == 1, two, three))
+            part_out[i, width : width + 16, :] = stats.astype(jnp.bfloat16)
+            p_copy(i).start()
+
+    def block_of(owner, i):
+        at = (owner * groups * PARTS + i) * part_heads * width
+        return o_ref.at[:, pl.ds(pl.multiple_of(at, part_heads * width), part_heads * width)]
+
+    def o_copy(owner, i, slot, target):
+        return pltpu.make_async_remote_copy(
+            src_ref=block_of(owner, i),
+            dst_ref=block_of(owner, i),
+            send_sem=o_send.at[slot, i],
+            recv_sem=o_recv.at[owner, i],
+            device_id={"head": target},
+            device_id_type=MESH,
+        )
+
+    def combine(i):
+        g, c = divmod(i, PARTS)
+        cols = slice(c * part_rows, (c + 1) * part_rows)
+        sums = total[2 * g, :, cols]
+        mine = high[2 * g, :, cols] + jnp.log(sums) * LOG2E
+        p_copy(i).wait_recv()
+        stats = part_in[i, width : width + 16, :].astype(jnp.float32)
+        theirs = stats[0:1] + stats[1:2] + stats[2:3]
+        top = jnp.maximum(mine, theirs)
+        a = jnp.exp2(mine - top)
+        b = jnp.exp2(theirs - top)
+        both = a + b
+        out = acc[2 * g, :, cols] * (a / (sums * both)) + part_in[i, 0:width, :].astype(
+            jnp.float32
+        ) * (b / both)
+        out = out.T
+        at = (me * groups * PARTS + i) * part_heads * width
+        for j in range(part_heads):
+            spot = pl.multiple_of(at + j * width, width)
+            o_ref[:, pl.ds(spot, width)] = out[j * fresh : (j + 1) * fresh].astype(jnp.bfloat16)
+        for k, peer in enumerate(peers):
+            o_copy(me, i, 1 + k, peer).start()
+        o_copy(me, i, 0, sibling).start()
+
+    def forward(i):
+        for k, peer in enumerate(peers):
+            o_copy(peer, i, 0, sibling).wait_recv()
+            o_copy(peer, i, 1 + len(peers) + k, sibling).start()
+
+    steps = groups * last
+
+    def body(it, carry):
+        apart = it // groups + 1
+        step(apart, it % groups, apart == 1)
+        return carry
+
+    lax.fori_loop(0, steps - groups + 1, body, 0)
+    finish(0)
+    for g in range(1, groups):
+        step(last, g, last == 1)
+        finish(g)
+
+    count = groups * PARTS
+    behind = PARTS
+    for i in range(count):
+        combine(i)
+        if i >= behind:
+            forward(i - behind)
+    for i in range(count - behind, count):
+        forward(i)
+    for i in range(count):
+        o_copy(sibling, i, 0, sibling).wait_recv()
+        for peer in peers:
+            far = peer + 1 - 2 * (peer % 2)
+            o_copy(far, i, 0, sibling).wait_recv()
+
+    for g in range(groups):
+        for src in range(column):
+
+            @pl.when(jnp.logical_and(has_up, src <= place))
+            def _():
+                up(src, g).wait_send()
+
+            @pl.when(jnp.logical_and(has_down, src >= place))
+            def _():
+                down(src, g).wait_send()
+
+        q_copy(g).wait_send()
+    for i in range(count):
+        p_copy(i).wait_send()
+        o_copy(me, i, 0, sibling).wait_send()
+        for k, peer in enumerate(peers):
+            o_copy(me, i, 1 + k, peer).wait_send()
+            o_copy(peer, i, 1 + len(peers) + k, sibling).wait_send()
+
+
+def in_one_kernel(queries, cache_keys, cache_values, new_keys, new_values, frame_of_slot, slopes):
+    fresh, local, width = queries.shape
+    cached, groups, _ = cache_keys.shape
+    group = local // groups
+    shards = lax.axis_size("ctx")
+    heads = lax.axis_size("head")
+    column = shards // 2
+    rows = group * fresh
+    slab = 2 * (cached + fresh) + 16
+    count = groups * PARTS
+    vmem = pl.BlockSpec(memory_space=pltpu.VMEM)
+    smem = pl.BlockSpec(memory_space=pltpu.SMEM)
+    dma = pltpu.SemaphoreType.DMA
+    sizes = (cached, fresh, groups, group, width, shards, heads)
+    return pl.pallas_call(
+        functools.partial(kernel, sizes),
+        out_shape=jax.ShapeDtypeStruct((fresh, heads * local * width), jnp.bfloat16),
+        in_specs=[vmem] * 5 + [smem] * 2,
+        out_specs=vmem,
+        scratch_shapes=[
+            pltpu.VMEM((column, groups, slab, width), jnp.bfloat16),
+            pltpu.VMEM((2, column * fresh, width), jnp.bfloat16),
+            pltpu.VMEM((2, groups, rows, width), jnp.bfloat16),
+            pltpu.VMEM((2 * groups, width, rows), jnp.float32),
+            pltpu.VMEM((2 * groups, 1, rows), jnp.float32),
+            pltpu.VMEM((2 * groups, 1, rows), jnp.float32),
+            pltpu.VMEM((count, width + 16, rows // PARTS), jnp.bfloat16),
+            pltpu.VMEM((count, width + 16, rows // PARTS), jnp.bfloat16),
+            dma((column, groups)),
+            dma((column, groups)),
+            dma((column, groups)),
+            dma((groups,)),
+            dma((groups,)),
+            dma((count,)),
+            dma((count,)),
+            dma((heads - 1, count)),
+            dma((heads, count)),
+        ],
+        compiler_params=pltpu.CompilerParams(
+            collective_id=0, has_side_effects=True, vmem_limit_bytes=48 * 1024 * 1024
+        ),
+        name="attend_over_slice",
+    )(
+        queries.reshape(fresh * local, width),
+        cache_keys.reshape(cached * groups, width),
+        cache_values.reshape(cached * groups, width),
+        new_keys.reshape(fresh * groups, width),
+        new_values.reshape(fresh * groups, width),
+        frame_of_slot,
+        slopes,
+    )
 
 
 def from_partner(value, axis, apart):
@@ -72,7 +489,7 @@
     return jnp.sum(acc * scaling[..., None], axis=0) / jnp.sum(total * scaling, axis=0)[..., None]
 
 
-def on_device(queries, cache_keys, cache_values, new_keys, new_values, frame_of_slot, slopes):
+def in_steps(queries, cache_keys, cache_values, new_keys, new_values, frame_of_slot, slopes):
     rows, local_heads, width = queries.shape
     groups = cache_keys.shape[1]
     group = local_heads // groups
@@ -146,6 +563,18 @@
     return lax.all_gather(result, "head", axis=1, tiled=True)
 
 
+def on_device(*arrays):
+    fresh, local, width = arrays[0].shape
+    cached = arrays[1].shape[0]
+    frames = arrays[5].shape[0]
+    shards, heads = lax.axis_size("ctx"), lax.axis_size("head")
+    whole_tiles = fresh % 16 == 0 and cached % 16 == 0 and width % 128 == 0
+    pairs = shards % 2 == 0 and shards > 2 and heads % 2 == 0
+    if whole_tiles and pairs and frames == 1 and (local // arrays[1].shape[1]) % PARTS == 0:
+        return in_one_kernel(*arrays)
+    return in_steps(*arrays)
+
+
 def solution(mesh):
     return jax.shard_map(
         on_device,

time: 170 us -> 46.6 us (0.27)
  waiting for transfers between devices: 74.6 us -> 0 us
  Pallas kernels: 0 us -> 39.7 us
  starting transfers between devices: 26.3 us -> 0 us
  local copies, waits for them, and re-layouts: 23.4 us -> 5.89 us
  other arithmetic: 16.2 us -> 0 us
  between operations: 14.4 us -> 0.67 us
  matrix products: 13 us -> 0 us
    all_to_all x4 -> x0, waiting for transfers between devices: 56.5 us -> none  [the longest x1 44.4 us: on_device(): lax.all_to_all(acc, 'ctx', split_axis=0, concat_axis=0, tiled=True)]
    pallas_call x0 -> x1, Pallas kernels: none -> 39.7 us  [in_one_kernel(): pl.pallas_call(functools.partial(kernel, sizes), out_shape=jax.ShapeDtype...]
    all_to_all x4 -> x0, starting transfers between devices: 20.1 us -> none  [the longest x1 7.38 us: on_device(): lax.all_to_all(outgoing, 'ctx', split_axis=0, concat_axis=0, tiled=True)]
    all_gather x1 -> x0, waiting for transfers between devices: 15.9 us -> none  [on_device(): return lax.all_gather(result, 'head', axis=1, tiled=True)]
    dot_general x6 -> x0, matrix products: 13 us -> none  [the longest x3 6.25 us: update(): jnp.einsum('rgqk,kgd->rgqd', weight, values, preferred_element_type=jnp.f...]
    reduce_sum x5 -> x0, other arithmetic: 7.48 us -> none  [the longest x3 6.69 us: update(): total = total * corr + jnp.sum(expo, axis=-1)]
    ppermute x5 -> x0, starting transfers between devices: 6.15 us -> none  [from_partner(): lax.ppermute(value, axis, [(i, i ^ 1 << apart) for i in range(lax.axis_si...]
    unnamed x41 -> x13, local copies, waits for them, and re-layouts: 10.8 us -> 5.89 us
  transfers between devices with their start and end apart: 10 -> 0, of which waited for: 6 -> 0; matrix products, arithmetic and copies ran while one was open for 24% -> 0% of each run, Pallas kernels for 0% -> 0%
where the time goes in v1:
time: 46.6 us; the launch traced here: 46.3 us
  Pallas kernels  39.7 us (85%)
  local copies, waits for them, and re-layouts  5.89 us (13%)
  between operations  0.67 us (1%)
    pallas_call x1, Pallas kernels, in_one_kernel(): pl.pallas_call(functools.partial(kernel, sizes), out_shape=jax.ShapeDtype...  39.7 us
    unnamed x13, local copies, waits for them, and re-layouts  5.89 us

profile of v1, /device:TPU:0, one launch (start us, length us, event | category | flops | bytes accessed | tf_op | source)
XLA Modules:
  0.0 46.3 jit_solution(4050959141005758429)
XLA Ops:
  0.7 0.0 copy-start.5
  0.7 0.6 %copy-done.5 = f32[16]{0:T(128)S(1)} copy-done((f32[16]{0:T(128)S(1)}, f32[16]{0:T(128)}, u32[]{:S(2)}) %copy-start.5) | copy-done | bytes 88
  1.3 0.0 copy-start
  1.3 0.9 %copy-done = bf16[64,16,128]{2,1,0:T(8,128)(2,1)S(1)} copy-done((bf16[64,16,128]{2,1,0:T(8,128)(2,1)S(1)}, bf16[64,16,128]{2,1,0:T(8,128)(2,1)}, u32[]{:S(2)}) %copy-start) | copy-done | bytes 262168
  2.3 0.0 copy-start.1
  2.3 0.9 %copy-done.1 = bf16[256,2,128]{2,1,0:T(2,128)(2,1)S(1)} copy-done((bf16[256,2,128]{2,1,0:T(2,128)(2,1)S(1)}, bf16[256,2,128]{2,1,0:T(2,128)(2,1)}, u32[]{:S(2)}) %copy-start.1) | copy-done | bytes 131096
  3.2 0.0 copy-start.2
  3.2 0.9 %copy-done.2 = bf16[256,2,128]{2,1,0:T(2,128)(2,1)S(1)} copy-done((bf16[256,2,128]{2,1,0:T(2,128)(2,1)S(1)}, bf16[256,2,128]{2,1,0:T(2,128)(2,1)}, u32[]{:S(2)}) %copy-start.2) | copy-done | bytes 131096
  4.1 0.0 copy-start.3
  4.1 0.8 %copy-done.3 = bf16[64,2,128]{2,1,0:T(2,128)(2,1)S(1)} copy-done((bf16[64,2,128]{2,1,0:T(2,128)(2,1)S(1)}, bf16[64,2,128]{2,1,0:T(2,128)(2,1)}, u32[]{:S(2)}) %copy-start.3) | copy-done | bytes 32792
  4.8 0.0 copy-start.4
  4.8 0.8 %copy-done.4 = bf16[64,2,128]{2,1,0:T(2,128)(2,1)S(1)} copy-done((bf16[64,2,128]{2,1,0:T(2,128)(2,1)S(1)}, bf16[64,2,128]{2,1,0:T(2,128)(2,1)}, u32[]{:S(2)}) %copy-start.4) | copy-done | bytes 32792
  5.6 39.7 %attend_over_slice.1 = bf16[64,8192]{1,0:T(8,128)(2,1)S(1)} custom-call(bf16[1024,128]{1,0:T(8,128)(2,1)S(1)} %bitcast.5, bf16[512,128]{1,0:T(8,128)(2,1)S(1)} %bitcast.6, bf16[512,128]{1,0:T(8,128)(2,1)S(1)} %bitcast.7, bf16[128,128]{1,0:T(8,128)(2,1)S(1)} %bitcast.8, bf16[128,128]{1,0:T(8,128)(2,1)S(1)} %bitcast.9, s32[1]{0:T(128)S(6)} %copy.9.frame_ref, ...), custom_call_target="tpu_custom_call" | custom-call | tf_op jit(solution)/shard_map/attend_over_slice/pallas_call | solution.py:387
  45.3 1.0 %copy.10 = bf16[64,8192]{1,0:T(8,128)(2,1)} copy(bf16[64,8192]{1,0:T(8,128)(2,1)S(1)} %attend_over_slice.1) | data formatting | bytes 2097152
Async XLA Ops:
  0.7 0.7 %copy-start.5 = (f32[16]{0:T(128)S(1)}, f32[16]{0:T(128)}, u32[]{:S(2)}) copy-start(f32[16]{0:T(128)} %slope_ref.1) | copy-start | bytes 196
  1.3 0.9 %copy-start = (bf16[64,16,128]{2,1,0:T(8,128)(2,1)S(1)}, bf16[64,16,128]{2,1,0:T(8,128)(2,1)}, u32[]{:S(2)}) copy-start(bf16[64,16,128]{2,1,0:T(8,128)(2,1)} %param.7) | copy-start | bytes 786436
  2.3 0.9 %copy-start.1 = (bf16[256,2,128]{2,1,0:T(2,128)(2,1)S(1)}, bf16[256,2,128]{2,1,0:T(2,128)(2,1)}, u32[]{:S(2)}) copy-start(bf16[256,2,128]{2,1,0:T(2,128)(2,1)} %param.8) | copy-start | bytes 393220
  3.2 0.9 %copy-start.2 = (bf16[256,2,128]{2,1,0:T(2,128)(2,1)S(1)}, bf16[256,2,128]{2,1,0:T(2,128)(2,1)}, u32[]{:S(2)}) copy-start(bf16[256,2,128]{2,1,0:T(2,128)(2,1)} %param.9) | copy-start | bytes 393220
  4.1 0.8 %copy-start.3 = (bf16[64,2,128]{2,1,0:T(2,128)(2,1)S(1)}, bf16[64,2,128]{2,1,0:T(2,128)(2,1)}, u32[]{:S(2)}) copy-start(bf16[64,2,128]{2,1,0:T(2,128)(2,1)} %param.10) | copy-start | bytes 98308
  4.8 0.8 %copy-start.4 = (bf16[64,2,128]{2,1,0:T(2,128)(2,1)S(1)}, bf16[64,2,128]{2,1,0:T(2,128)(2,1)}, u32[]{:S(2)}) copy-start(bf16[64,2,128]{2,1,0:T(2,128)(2,1)} %param.11) | copy-start | bytes 98308

commit v2 on v1

--- a/solution.py
+++ b/solution.py
@@ -9,6 +9,7 @@
 from jax.sharding import PartitionSpec as P
 
 FRAME = 256
+FRAME_BITS = FRAME.bit_length() - 1
 MESH = pl.DeviceIdType.MESH
 LOG2E = 1.0 / math.log(2.0)
 PARTS = 2
@@ -28,6 +29,14 @@
 
 def kernel(
     sizes,
+    q_in,
+    ck_in,
+    cv_in,
+    nk_in,
+    nv_in,
+    frame_in,
+    slope_in,
+    o_ref,
     q_ref,
     ck_ref,
     cv_ref,
@@ -35,15 +44,15 @@
     nv_ref,
     frame_ref,
     slope_ref,
-    o_ref,
     kv,
-    newkv,
     qb,
+    slope_rows,
     acc,
     high,
     total,
     part_out,
     part_in,
+    in_sem,
     kv_up,
     kv_down,
     kv_recv,
@@ -72,6 +81,23 @@
     v_at = cached + fresh
     f_at = 2 * v_at
 
+    fetches = [
+        pltpu.make_async_copy(src, dst, in_sem.at[k])
+        for k, (src, dst) in enumerate(
+            (
+                (ck_in, ck_ref),
+                (nk_in, nk_ref),
+                (cv_in, cv_ref),
+                (nv_in, nv_ref),
+                (frame_in, frame_ref),
+                (q_in, q_ref),
+                (slope_in, slope_ref),
+            )
+        )
+    ]
+    for fetch in fetches:
+        fetch.start()
+
     barrier = pltpu.get_barrier_semaphore()
     pl.semaphore_signal(barrier, inc=1, device_id={"ctx": across}, device_id_type=MESH)
     for other in [sibling] + peers:
@@ -85,6 +111,8 @@
     def _():
         pl.semaphore_signal(barrier, inc=1, device_id={"ctx": position - 2}, device_id_type=MESH)
 
+    for fetch in fetches[:5]:
+        fetch.wait()
     frame = frame_ref[0].astype(jnp.float32)
     for g in range(groups):
         pick = (iota((cached, groups * cached), 1) == groups * iota((cached, groups * cached), 0) + g)
@@ -147,78 +175,76 @@
             device_id_type=MESH,
         )
 
+    for fetch in fetches[5:]:
+        fetch.wait()
     local = groups * group
+    slant = iota((fresh, local * fresh), 1) - local * iota((fresh, local * fresh), 0)
     for g in range(groups):
-        r = iota((rows, local * fresh), 0)
-        want = (r % fresh) * local + r // fresh + g * group
-        pick = (iota((rows, local * fresh), 1) == want).astype(jnp.float32).astype(jnp.bfloat16)
+        pick = jnp.concatenate(
+            [
+                (slant == g * group + j).astype(jnp.float32).astype(jnp.bfloat16)
+                for j in range(group)
+            ],
+            axis=0,
+        )
         qb[0, g] = jnp.dot(pick, q_ref[...], preferred_element_type=jnp.float32).astype(jnp.bfloat16)
         q_copy(g).start()
 
-    lane = iota((1, rows), 1)
-    token = lane % fresh
-
-    def slope_row(g):
-        head = lane // fresh
-        row = jnp.zeros((1, rows), jnp.float32)
-        for j in range(group):
-            row = jnp.where(head == j, slope_ref[g * group + j], row)
-        return row * LOG2E
+    token = iota((1, rows), 1)
+    for g in range(groups):
+        row = jnp.full((1, rows), slope_ref[g * group])
+        for j in range(1, group):
+            row = jnp.where(token >= j * fresh, slope_ref[g * group + j], row)
+        slope_rows[g] = row * LOG2E
+    for j in range(group - 1, 0, -1):
+        token = jnp.where(token >= j * fresh, token - j * fresh, token)
 
     def query_position(r):
         owner = position if r == 0 else across
         return owner * fresh + token
 
-    def query_frame(r):
-        return (cache_frames + query_position(r) // FRAME).astype(jnp.float32)
+    def frame_of(positions):
+        return (cache_frames + jnp.right_shift(positions, FRAME_BITS)).astype(jnp.float32)
 
     for i in range(2 * groups):
         acc[i] = jnp.zeros((width, rows), jnp.float32)
         high[i] = jnp.full((1, rows), -1e30, jnp.float32)
         total[i] = jnp.zeros((1, rows), jnp.float32)
 
-    def update(i, score, shift, values):
-        before = high[i]
-        now = jnp.maximum(before, jnp.max(score, axis=0, keepdims=True) + shift)
-        corr = jnp.exp2(before - now)
-        expo = jnp.exp2(score + (shift - now))
-        high[i] = now
-        total[i] = total[i] * corr + jnp.sum(expo, axis=0, keepdims=True)
-        acc[i] = acc[i] * corr + tn(values, expo.astype(jnp.bfloat16))
-
-    def slopes_of(g):
-        if isinstance(g, int):
-            return slope_row(g)
-        row = slope_row(0)
-        for k in range(1, groups):
-            row = jnp.where(g == k, slope_row(k), row)
-        return row
-
-    def attend(src, g):
-        keys = kv[src, g, 0:cached, :]
-        values = kv[src, g, v_at : v_at + cached, :]
+    def attend(src, g, sides=(1, 0)):
+        keys = kv[src, g, 0:v_at, :]
+        values = kv[src, g, v_at:f_at, :]
         key_frame = kv[src, g, f_at : f_at + 16, :].astype(jnp.float32)[0:1, 0:1]
-        slope = slopes_of(g)
-        for r in (1, 0):
+        key_position = iota((fresh, 1), 0) + (2 * src + side) * fresh
+        new_frame = frame_of(key_position)
+        slope = slope_rows[g]
+        before = [(high[2 * g + r], total[2 * g + r], acc[2 * g + r]) for r in sides]
+        after = []
+        for r, (top, sums, out) in zip(sides, before):
             score = nt(keys, qb[r, g]) * scale
-            update(2 * g + r, score, -slope * (query_frame(r) - key_frame), values)
-
-    def attend_new(g):
-        for src in range(column):
-            newkv[0, src * fresh : (src + 1) * fresh, :] = kv[src, g, cached : cached + fresh, :]
-            newkv[1, src * fresh : (src + 1) * fresh, :] = kv[
-                src, g, v_at + cached : v_at + cached + fresh, :
-            ]
-        index = iota((column * fresh, 1), 0)
-        key_position = ((index // fresh) * 2 + side) * fresh + index % fresh
-        key_frame = (cache_frames + key_position // FRAME).astype(jnp.float32)
-        slope = slope_row(g)
-        for r in (1, 0):
-            score = nt(newkv[0], qb[r, g]) * scale - slope * (query_frame(r) - key_frame)
-            score = jnp.where(key_position <= query_position(r), score, -1e30)
-            update(2 * g + r, score, jnp.zeros((1, rows), jnp.float32), newkv[1])
-
-    def step(apart, g, first):
+            here = query_position(r)
+            shift = slope * (key_frame - frame_of(here))
+            old = score[:cached]
+            new = score[cached:] + slope * (new_frame - frame_of(here))
+            new = jnp.where(key_position <= here, new, -1e30)
+            now = jnp.maximum(
+                jnp.max(old, axis=0, keepdims=True) + shift, jnp.max(new, axis=0, keepdims=True)
+            )
+            now = jnp.maximum(top, now)
+            corr = jnp.exp2(top - now)
+            old = jnp.exp2(old + (shift - now))
+            new = jnp.exp2(new - now)
+            sums = sums * corr + (
+                jnp.sum(old, axis=0, keepdims=True) + jnp.sum(new, axis=0, keepdims=True)
+            )
+            weight = jnp.concatenate([old.astype(jnp.bfloat16), new.astype(jnp.bfloat16)], axis=0)
+            after.append((now, sums, out * corr + tn(values, weight)))
+        for r, (now, sums, out) in zip(sides, after):
+            high[2 * g + r] = now
+            total[2 * g + r] = sums
+            acc[2 * g + r] = out
+
+    def pass_on(apart, g):
         low = place - apart
         top = place + apart
 
@@ -238,18 +264,17 @@
             def _():
                 down(top, g).start()
 
-        @pl.when(first)
-        def _():
-            q_copy(g).wait_recv()
-            attend(place, g)
+    def attend_pair(apart, g, sides=(1, 0)):
+        low = place - apart
+        top = place + apart
 
         @pl.when(low >= 0)
         def _():
-            attend(low, g)
+            attend(low, g, sides)
 
         @pl.when(top <= last)
         def _():
-            attend(top, g)
+            attend(top, g, sides)
 
     part_rows = rows // PARTS
     part_heads = group // PARTS
@@ -265,13 +290,12 @@
         )
 
     def finish(g):
-        attend_new(g)
         sub = iota((16, part_rows), 0)
         for c in range(PARTS):
             i = g * PARTS + c
             cols = slice(c * part_rows, (c + 1) * part_rows)
             sums = total[2 * g + 1, :, cols]
-            part_out[i, 0:width, :] = (acc[2 * g + 1, :, cols] / sums).astype(jnp.bfloat16)
+            part_out[i, 0:width, :] = (acc[2 * g + 1, :, cols] * (1.0 / sums)).astype(jnp.bfloat16)
             lse = high[2 * g + 1, :, cols] + jnp.log(sums) * LOG2E
             one = lse.astype(jnp.bfloat16).astype(jnp.float32)
             two = (lse - one).astype(jnp.bfloat16).astype(jnp.float32)
@@ -327,14 +351,24 @@
 
     def body(it, carry):
         apart = it // groups + 1
-        step(apart, it % groups, apart == 1)
+        g = it % groups
+        pass_on(apart, g)
+
+        @pl.when(apart == 1)
+        def _():
+            q_copy(g).wait_recv()
+            attend(place, g)
+
+        attend_pair(apart, g)
         return carry
 
     lax.fori_loop(0, steps - groups + 1, body, 0)
     finish(0)
     for g in range(1, groups):
-        step(last, g, last == 1)
+        pass_on(last, g)
+        attend_pair(last, g, (1,))
         finish(g)
+        attend_pair(last, g, (0,))
 
     count = groups * PARTS
     behind = PARTS
@@ -381,23 +415,30 @@
     slab = 2 * (cached + fresh) + 16
     count = groups * PARTS
     vmem = pl.BlockSpec(memory_space=pltpu.VMEM)
-    smem = pl.BlockSpec(memory_space=pltpu.SMEM)
     dma = pltpu.SemaphoreType.DMA
     sizes = (cached, fresh, groups, group, width, shards, heads)
     return pl.pallas_call(
         functools.partial(kernel, sizes),
         out_shape=jax.ShapeDtypeStruct((fresh, heads * local * width), jnp.bfloat16),
-        in_specs=[vmem] * 5 + [smem] * 2,
+        in_specs=[pl.BlockSpec(memory_space=pl.ANY)] * 7,
         out_specs=vmem,
         scratch_shapes=[
+            pltpu.VMEM((fresh * local, width), jnp.bfloat16),
+            pltpu.VMEM((cached * groups, width), jnp.bfloat16),
+            pltpu.VMEM((cached * groups, width), jnp.bfloat16),
+            pltpu.VMEM((fresh * groups, width), jnp.bfloat16),
+            pltpu.VMEM((fresh * groups, width), jnp.bfloat16),
+            pltpu.SMEM(frame_of_slot.shape, jnp.int32),
+            pltpu.SMEM(slopes.shape, jnp.float32),
             pltpu.VMEM((column, groups, slab, width), jnp.bfloat16),
-            pltpu.VMEM((2, column * fresh, width), jnp.bfloat16),
             pltpu.VMEM((2, groups, rows, width), jnp.bfloat16),
+            pltpu.VMEM((groups, 1, rows), jnp.float32),
             pltpu.VMEM((2 * groups, width, rows), jnp.float32),
             pltpu.VMEM((2 * groups, 1, rows), jnp.float32),
             pltpu.VMEM((2 * groups, 1, rows), jnp.float32),
             pltpu.VMEM((count, width + 16, rows // PARTS), jnp.bfloat16),
             pltpu.VMEM((count, width + 16, rows // PARTS), jnp.bfloat16),
+            dma((7,)),
             dma((column, groups)),
             dma((column, groups)),
             dma((column, groups)),
@@ -409,7 +450,7 @@
             dma((heads, count)),
         ],
         compiler_params=pltpu.CompilerParams(
-            collective_id=0, has_side_effects=True, vmem_limit_bytes=48 * 1024 * 1024
+            collective_id=0, has_side_effects=True, vmem_limit_bytes=64 * 1024 * 1024
         ),
         name="attend_over_slice",
     )(

time: 46.6 us -> 42.5 us (0.912)
  local copies, waits for them, and re-layouts: 5.89 us -> 2.26 us
    unnamed x13 -> x1, local copies, waits for them, and re-layouts: 5.89 us -> 2.26 us
where the time goes in v2:
time: 42.5 us; the launch traced here: 42.3 us
  Pallas kernels  39.4 us (93%)
  local copies, waits for them, and re-layouts  2.26 us (5%)
  between operations  0.66 us (2%)
    pallas_call x1, Pallas kernels, in_one_kernel(): pl.pallas_call(functools.partial(kernel, sizes), out_shape=jax.ShapeDtype...  39.4 us
    unnamed x1, local copies, waits for them, and re-layouts  2.26 us

profile of v2, /device:TPU:0, one launch (start us, length us, event | category | flops | bytes accessed | tf_op | source)
XLA Modules:
  0.0 42.3 jit_solution(4853027078414531860)
XLA Ops:
  0.7 39.4 %attend_over_slice.1 = bf16[64,8192]{1,0:T(8,128)(2,1)} custom-call(bf16[1024,128]{1,0:T(8,128)(2,1)} %bitcast.5, bf16[512,128]{1,0:T(8,128)(2,1)} %bitcast.6, bf16[512,128]{1,0:T(8,128)(2,1)} %bitcast.7, bf16[128,128]{1,0:T(8,128)(2,1)} %bitcast.8, bf16[128,128]{1,0:T(8,128)(2,1)} %bitcast.9, s32[1]{0:T(128)S(6)} %copy.9.frame_in, f32[16]{0:T(128)} %slope_in.1), custom_call_target="tpu_custom_call" | custom-call | tf_op jit(solution)/shard_map/attend_over_slice/pallas_call | solution.py:420
  40.1 2.3 %copy.10 = bf16[64,8192]{1,0:T(8,128)(2,1)} copy(bf16[64,8192]{1,0:T(8,128)(2,1)} %attend_over_slice.1) | data formatting | bytes 2097152

commit v3 on v2

--- a/solution.py
+++ b/solution.py
@@ -12,15 +12,11 @@
 FRAME_BITS = FRAME.bit_length() - 1
 MESH = pl.DeviceIdType.MESH
 LOG2E = 1.0 / math.log(2.0)
-PARTS = 2
+PARTS = 4
 
 
 def nt(a, b):
     return lax.dot_general(a, b, (((1,), (1,)), ((), ())), preferred_element_type=jnp.float32)
-
-
-def tn(a, b):
-    return lax.dot_general(a, b, (((0,), (0,)), ((), ())), preferred_element_type=jnp.float32)
 
 
 def iota(shape, dim):
@@ -78,8 +74,11 @@
     has_up = place < last
     has_down = place > 0
     scale = LOG2E / width**0.5
-    v_at = cached + fresh
-    f_at = 2 * v_at
+    k_at = fresh
+    f_at = fresh + cached
+    v_at = f_at + 16
+    n_at = v_at + cached
+    old_rows = slice(k_at, n_at)
 
     fetches = [
         pltpu.make_async_copy(src, dst, in_sem.at[k])
@@ -111,30 +110,6 @@
     def _():
         pl.semaphore_signal(barrier, inc=1, device_id={"ctx": position - 2}, device_id_type=MESH)
 
-    for fetch in fetches[:5]:
-        fetch.wait()
-    frame = frame_ref[0].astype(jnp.float32)
-    for g in range(groups):
-        pick = (iota((cached, groups * cached), 1) == groups * iota((cached, groups * cached), 0) + g)
-        pick = pick.astype(jnp.float32).astype(jnp.bfloat16)
-        few = pick[:fresh, : groups * fresh]
-        for src, at, sel, n in (
-            (ck_ref, 0, pick, cached),
-            (nk_ref, cached, few, fresh),
-            (cv_ref, v_at, pick, cached),
-            (nv_ref, v_at + cached, few, fresh),
-        ):
-            kv[place, g, at : at + n, :] = jnp.dot(
-                sel, src[...], preferred_element_type=jnp.float32
-            ).astype(jnp.bfloat16)
-        kv[place, g, f_at : f_at + 16, :] = jnp.full((16, width), frame, jnp.float32).astype(
-            jnp.bfloat16
-        )
-
-    pl.semaphore_wait(
-        barrier, 1 + heads // 2 + jnp.minimum(place, 1) + jnp.minimum(last - place, 1)
-    )
-
     def up(src, g):
         return pltpu.make_async_remote_copy(
             src_ref=kv.at[src, g],
@@ -147,15 +122,35 @@
 
     def down(src, g):
         return pltpu.make_async_remote_copy(
-            src_ref=kv.at[src, g],
-            dst_ref=kv.at[src, g],
+            src_ref=kv.at[src, g, old_rows],
+            dst_ref=kv.at[src, g, old_rows],
             send_sem=kv_down.at[src, g],
             recv_sem=kv_recv.at[src, g],
             device_id={"ctx": position - 2},
             device_id_type=MESH,
         )
 
+    for fetch in fetches[:5]:
+        fetch.wait()
+    frame = frame_ref[0].astype(jnp.float32)
+    slant = iota((cached, groups * cached), 1) - groups * iota((cached, groups * cached), 0)
     for g in range(groups):
+        pick = (slant == g).astype(jnp.float32).astype(jnp.bfloat16)
+        few = pick[:fresh, : groups * fresh]
+        for src, at, sel, n in (
+            (nk_ref, 0, few, fresh),
+            (ck_ref, k_at, pick, cached),
+            (cv_ref, v_at, pick, cached),
+            (nv_ref, n_at, few, fresh),
+        ):
+            kv[place, g, at : at + n, :] = jnp.dot(
+                sel, src[...], preferred_element_type=jnp.float32
+            ).astype(jnp.bfloat16)
+        kv[place, g, f_at:v_at, :] = jnp.full((16, width), frame, jnp.float32).astype(jnp.bfloat16)
+        if g == 0:
+            pl.semaphore_wait(
+                barrier, 1 + heads // 2 + jnp.minimum(place, 1) + jnp.minimum(last - place, 1)
+            )
 
         @pl.when(has_up)
         def _():
@@ -211,10 +206,10 @@
         high[i] = jnp.full((1, rows), -1e30, jnp.float32)
         total[i] = jnp.zeros((1, rows), jnp.float32)
 
-    def attend(src, g, sides=(1, 0)):
-        keys = kv[src, g, 0:v_at, :]
-        values = kv[src, g, v_at:f_at, :]
-        key_frame = kv[src, g, f_at : f_at + 16, :].astype(jnp.float32)[0:1, 0:1]
+    def attend(src, g, sides, seen):
+        keys = kv[src, g, 0 if seen else k_at : f_at, :]
+        values = kv[src, g, v_at : n_at + fresh if seen else n_at, :].T
+        key_frame = kv[src, g, f_at:v_at, :].astype(jnp.float32)[0:1, 0:1]
         key_position = iota((fresh, 1), 0) + (2 * src + side) * fresh
         new_frame = frame_of(key_position)
         slope = slope_rows[g]
@@ -224,21 +219,22 @@
             score = nt(keys, qb[r, g]) * scale
             here = query_position(r)
             shift = slope * (key_frame - frame_of(here))
-            old = score[:cached]
-            new = score[cached:] + slope * (new_frame - frame_of(here))
-            new = jnp.where(key_position <= here, new, -1e30)
-            now = jnp.maximum(
-                jnp.max(old, axis=0, keepdims=True) + shift, jnp.max(new, axis=0, keepdims=True)
-            )
-            now = jnp.maximum(top, now)
+            old = score[fresh:] if seen else score
+            now = jnp.maximum(top, jnp.max(old, axis=0, keepdims=True) + shift)
+            if seen:
+                new = score[:fresh] + slope * (new_frame - frame_of(here))
+                new = jnp.where(key_position <= here, new, -1e30)
+                now = jnp.maximum(now, jnp.max(new, axis=0, keepdims=True))
             corr = jnp.exp2(top - now)
             old = jnp.exp2(old + (shift - now))
-            new = jnp.exp2(new - now)
-            sums = sums * corr + (
-                jnp.sum(old, axis=0, keepdims=True) + jnp.sum(new, axis=0, keepdims=True)
-            )
-            weight = jnp.concatenate([old.astype(jnp.bfloat16), new.astype(jnp.bfloat16)], axis=0)
-            after.append((now, sums, out * corr + tn(values, weight)))
+            fresh_sum = jnp.sum(old, axis=0, keepdims=True)
+            weight = old.astype(jnp.bfloat16)
+            if seen:
+                new = jnp.exp2(new - now)
+                fresh_sum = fresh_sum + jnp.sum(new, axis=0, keepdims=True)
+                weight = jnp.concatenate([weight, new.astype(jnp.bfloat16)], axis=0)
+            out = out * corr + jnp.dot(values, weight, preferred_element_type=jnp.float32)
+            after.append((now, sums * corr + fresh_sum, out))
         for r, (now, sums, out) in zip(sides, after):
             high[2 * g + r] = now
             total[2 * g + r] = sums
@@ -270,11 +266,11 @@
 
         @pl.when(low >= 0)
         def _():
-            attend(low, g, sides)
+            attend(low, g, sides, True)
 
         @pl.when(top <= last)
         def _():
-            attend(top, g, sides)
+            attend(top, g, sides, False)
 
     part_rows = rows // PARTS
     part_heads = group // PARTS
@@ -357,26 +353,29 @@
         @pl.when(apart == 1)
         def _():
             q_copy(g).wait_recv()
-            attend(place, g)
+            attend(place, g, (1,), True)
 
         attend_pair(apart, g)
         return carry
 
-    lax.fori_loop(0, steps - groups + 1, body, 0)
-    finish(0)
-    for g in range(1, groups):
+    for g in range(groups):
+        attend(place, g, (0,), True)
+    lax.fori_loop(0, steps - groups, body, 0)
+    for g in range(groups):
         pass_on(last, g)
         attend_pair(last, g, (1,))
         finish(g)
+        if g > 0:
+            for c in range(PARTS):
+                combine((g - 1) * PARTS + c)
         attend_pair(last, g, (0,))
 
     count = groups * PARTS
-    behind = PARTS
-    for i in range(count):
-        combine(i)
-        if i >= behind:
-            forward(i - behind)
-    for i in range(count - behind, count):
+    for c in range(PARTS):
+        combine(count - PARTS + c)
+        for g in range(groups - 1):
+            forward(g * PARTS + c)
+    for i in range(count - PARTS, count):
         forward(i)
     for i in range(count):
         o_copy(sibling, i, 0, sibling).wait_recv()
@@ -450,7 +449,7 @@
             dma((heads, count)),
         ],
         compiler_params=pltpu.CompilerParams(
-            collective_id=0, has_side_effects=True, vmem_limit_bytes=64 * 1024 * 1024
+            collective_id=0, has_side_effects=True, vmem_limit_bytes=62 * 1024 * 1024
         ),
         name="attend_over_slice",
     )(
@@ -610,7 +609,7 @@
     frames = arrays[5].shape[0]
     shards, heads = lax.axis_size("ctx"), lax.axis_size("head")
     whole_tiles = fresh % 16 == 0 and cached % 16 == 0 and width % 128 == 0
-    pairs = shards % 2 == 0 and shards > 2 and heads % 2 == 0
+    pairs = shards % 2 == 0 and shards > 4 and heads % 2 == 0
     if whole_tiles and pairs and frames == 1 and (local // arrays[1].shape[1]) % PARTS == 0:
         return in_one_kernel(*arrays)
     return in_steps(*arrays)

time: 42.5 us -> 40 us (0.941)
  the two profiles are of different devices: /device:TPU:0 before, /device:TPU:25 now
where the time goes in v3:
time: 40 us; the launch traced here: 39.8 us
  Pallas kernels  36.9 us (92%)
  local copies, waits for them, and re-layouts  2.26 us (6%)
  between operations  0.66 us (2%)
    pallas_call x1, Pallas kernels, in_one_kernel(): pl.pallas_call(functools.partial(kernel, sizes), out_shape=jax.ShapeDtype...  36.9 us
    unnamed x1, local copies, waits for them, and re-layouts  2.26 us

profile of v3, /device:TPU:25, one launch (start us, length us, event | category | flops | bytes accessed | tf_op | source)
XLA Modules:
  0.0 39.8 jit_solution(17458725570482379980)
XLA Ops:
  0.7 36.9 %attend_over_slice.1 = bf16[64,8192]{1,0:T(8,128)(2,1)} custom-call(bf16[1024,128]{1,0:T(8,128)(2,1)} %bitcast.5, bf16[512,128]{1,0:T(8,128)(2,1)} %bitcast.6, bf16[512,128]{1,0:T(8,128)(2,1)} %bitcast.7, bf16[128,128]{1,0:T(8,128)(2,1)} %bitcast.8, bf16[128,128]{1,0:T(8,128)(2,1)} %bitcast.9, s32[1]{0:T(128)S(6)} %copy.9.frame_in, f32[16]{0:T(128)} %slope_in.1), custom_call_target="tpu_custom_call" | custom-call | tf_op jit(solution)/shard_map/attend_over_slice/pallas_call | solution.py:419
  37.6 2.3 %copy.10 = bf16[64,8192]{1,0:T(8,128)(2,1)} copy(bf16[64,8192]{1,0:T(8,128)(2,1)} %attend_over_slice.1) | data formatting | bytes 2097152

commit v4 on v3

--- a/solution.py
+++ b/solution.py
@@ -78,7 +78,6 @@
     f_at = fresh + cached
     v_at = f_at + 16
     n_at = v_at + cached
-    old_rows = slice(k_at, n_at)
 
     fetches = [
         pltpu.make_async_copy(src, dst, in_sem.at[k])
@@ -110,25 +109,30 @@
     def _():
         pl.semaphore_signal(barrier, inc=1, device_id={"ctx": position - 2}, device_id_type=MESH)
 
-    def up(src, g):
+    pieces = ((0, v_at), (v_at, n_at + fresh))
+
+    def slab_copy(src, g, h, to_up):
+        start, stop = pieces[h]
+        if not to_up:
+            start, stop = max(start, k_at), min(stop, n_at)
+        ref = kv.at[src, g, start:stop]
         return pltpu.make_async_remote_copy(
-            src_ref=kv.at[src, g],
-            dst_ref=kv.at[src, g],
-            send_sem=kv_up.at[src, g],
-            recv_sem=kv_recv.at[src, g],
-            device_id={"ctx": position + 2},
+            src_ref=ref,
+            dst_ref=ref,
+            send_sem=(kv_up if to_up else kv_down).at[src, g, h],
+            recv_sem=kv_recv.at[src, g, h],
+            device_id={"ctx": position + 2 if to_up else position - 2},
             device_id_type=MESH,
         )
 
-    def down(src, g):
-        return pltpu.make_async_remote_copy(
-            src_ref=kv.at[src, g, old_rows],
-            dst_ref=kv.at[src, g, old_rows],
-            send_sem=kv_down.at[src, g],
-            recv_sem=kv_recv.at[src, g],
-            device_id={"ctx": position - 2},
-            device_id_type=MESH,
-        )
+    def send_own(g, h):
+        @pl.when(has_up)
+        def _():
+            slab_copy(place, g, h, True).start()
+
+        @pl.when(has_down)
+        def _():
+            slab_copy(place, g, h, False).start()
 
     for fetch in fetches[:5]:
         fetch.wait()
@@ -152,13 +156,9 @@
                 barrier, 1 + heads // 2 + jnp.minimum(place, 1) + jnp.minimum(last - place, 1)
             )
 
-        @pl.when(has_up)
-        def _():
-            up(place, g).start()
-
-        @pl.when(has_down)
-        def _():
-            down(place, g).start()
+        send_own(g, 0)
+        if g == 0:
+            send_own(g, 1)
 
     def q_copy(g):
         return pltpu.make_async_remote_copy(
@@ -246,19 +246,21 @@
 
         @pl.when(low >= 0)
         def _():
-            up(low, g).wait_recv()
-
-            @pl.when(has_up)
-            def _():
-                up(low, g).start()
+            for h in range(2):
+                slab_copy(low, g, h, True).wait_recv()
+
+                @pl.when(has_up)
+                def _():
+                    slab_copy(low, g, h, True).start()
 
         @pl.when(top <= last)
         def _():
-            down(top, g).wait_recv()
-
-            @pl.when(has_down)
-            def _():
-                down(top, g).start()
+            for h in range(2):
+                slab_copy(top, g, h, False).wait_recv()
+
+                @pl.when(has_down)
+                def _():
+                    slab_copy(top, g, h, False).start()
 
     def attend_pair(apart, g, sides=(1, 0)):
         low = place - apart
@@ -343,12 +345,14 @@
             o_copy(peer, i, 0, sibling).wait_recv()
             o_copy(peer, i, 1 + len(peers) + k, sibling).start()
 
-    steps = groups * last
-
-    def body(it, carry):
-        apart = it // groups + 1
-        g = it % groups
+    def body(k, carry):
+        g = jnp.where(k == 0, 0, 1 - k % 2)
+        apart = jnp.where(k == 0, 1, jnp.where(k % 2 == 1, (k + 3) // 2, k // 2))
         pass_on(apart, g)
+
+        @pl.when(k == 0)
+        def _():
+            send_own(1, 1)
 
         @pl.when(apart == 1)
         def _():
@@ -358,19 +362,22 @@
         attend_pair(apart, g)
         return carry
 
+    count = groups * PARTS
     for g in range(groups):
         attend(place, g, (0,), True)
-    lax.fori_loop(0, steps - groups, body, 0)
-    for g in range(groups):
-        pass_on(last, g)
-        attend_pair(last, g, (1,))
-        finish(g)
-        if g > 0:
-            for c in range(PARTS):
-                combine((g - 1) * PARTS + c)
-        attend_pair(last, g, (0,))
-
-    count = groups * PARTS
+    lax.fori_loop(0, 2 * last - 3, body, 0)
+    pass_on(last, 0)
+    attend_pair(last, 0, (1,))
+    finish(0)
+    attend_pair(last, 0, (0,))
+    pass_on(last - 1, 1)
+    attend_pair(last - 1, 1)
+    for c in range(PARTS):
+        combine(c)
+    pass_on(last, 1)
+    attend_pair(last, 1, (1,))
+    finish(1)
+    attend_pair(last, 1, (0,))
     for c in range(PARTS):
         combine(count - PARTS + c)
         for g in range(groups - 1):
@@ -388,11 +395,13 @@
 
             @pl.when(jnp.logical_and(has_up, src <= place))
             def _():
-                up(src, g).wait_send()
+                for h in range(2):
+                    slab_copy(src, g, h, True).wait_send()
 
             @pl.when(jnp.logical_and(has_down, src >= place))
             def _():
-                down(src, g).wait_send()
+                for h in range(2):
+                    slab_copy(src, g, h, False).wait_send()
 
         q_copy(g).wait_send()
     for i in range(count):
@@ -418,7 +427,7 @@
     sizes = (cached, fresh, groups, group, width, shards, heads)
     return pl.pallas_call(
         functools.partial(kernel, sizes),
-        out_shape=jax.ShapeDtypeStruct((fresh, heads * local * width), jnp.bfloat16),
+        out_shape=pltpu.VMEM((fresh, heads * local * width), jnp.bfloat16),
         in_specs=[pl.BlockSpec(memory_space=pl.ANY)] * 7,
         out_specs=vmem,
         scratch_shapes=[
@@ -438,9 +447,9 @@
             pltpu.VMEM((count, width + 16, rows // PARTS), jnp.bfloat16),
             pltpu.VMEM((count, width + 16, rows // PARTS), jnp.bfloat16),
             dma((7,)),
-            dma((column, groups)),
-            dma((column, groups)),
-            dma((column, groups)),
+            dma((column, groups, 2)),
+            dma((column, groups, 2)),
+            dma((column, groups, 2)),
             dma((groups,)),
             dma((groups,)),
             dma((count,)),
@@ -609,7 +618,7 @@
     frames = arrays[5].shape[0]
     shards, heads = lax.axis_size("ctx"), lax.axis_size("head")
     whole_tiles = fresh % 16 == 0 and cached % 16 == 0 and width % 128 == 0
-    pairs = shards % 2 == 0 and shards > 4 and heads % 2 == 0
+    pairs = shards % 2 == 0 and shards > 6 and heads % 2 == 0 and arrays[1].shape[1] == 2
     if whole_tiles and pairs and frames == 1 and (local // arrays[1].shape[1]) % PARTS == 0:
         return in_one_kernel(*arrays)
     return in_steps(*arrays)

time: 40 us -> 37.2 us (0.930)
  the two profiles are of different devices: /device:TPU:25 before, /device:TPU:0 now
where the time goes in v4:
time: 37.2 us; the launch traced here: 36.6 us
  Pallas kernels  35 us (94%)
  local copies, waits for them, and re-layouts  0.97 us (3%)
  between operations  0.66 us (2%)
    pallas_call x1, Pallas kernels, in_one_kernel(): pl.pallas_call(functools.partial(kernel, sizes), out_shape=pltpu.VMEM((fr...  35 us
    unnamed x1, local copies, waits for them, and re-layouts  0.97 us

profile of v4, /device:TPU:0, one launch (start us, length us, event | category | flops | bytes accessed | tf_op | source)
XLA Modules:
  0.0 36.6 jit_solution(16987526340276031232)
XLA Ops:
  0.7 35.0 %attend_over_slice.1 = bf16[64,8192]{1,0:T(8,128)(2,1)S(1)} custom-call(bf16[1024,128]{1,0:T(8,128)(2,1)} %bitcast.5, bf16[512,128]{1,0:T(8,128)(2,1)} %bitcast.6, bf16[512,128]{1,0:T(8,128)(2,1)} %bitcast.7, bf16[128,128]{1,0:T(8,128)(2,1)} %bitcast.8, bf16[128,128]{1,0:T(8,128)(2,1)} %bitcast.9, s32[1]{0:T(128)S(6)} %copy.10.frame_in, f32[16]{0:T(128)} %slope_in.1), custom_call_target="tpu_custom_call" | custom-call | tf_op jit(solution)/shard_map/attend_over_slice/pallas_call | solution.py:428
  35.7 1.0 %copy.9 = bf16[64,8192]{1,0:T(8,128)(2,1)} copy(bf16[64,8192]{1,0:T(8,128)(2,1)S(1)} %attend_over_slice.1) | data formatting | bytes 2097152

commit v5 on v4

--- a/solution.py
+++ b/solution.py
@@ -134,12 +134,13 @@
         def _():
             slab_copy(place, g, h, False).start()
 
+    slant = iota((cached, groups * cached), 1) - groups * iota((cached, groups * cached), 0)
+    picks = [(slant == g).astype(jnp.float32).astype(jnp.bfloat16) for g in range(groups)]
     for fetch in fetches[:5]:
         fetch.wait()
     frame = frame_ref[0].astype(jnp.float32)
-    slant = iota((cached, groups * cached), 1) - groups * iota((cached, groups * cached), 0)
     for g in range(groups):
-        pick = (slant == g).astype(jnp.float32).astype(jnp.bfloat16)
+        pick = picks[g]
         few = pick[:fresh, : groups * fresh]
         for src, at, sel, n in (
             (nk_ref, 0, few, fresh),
@@ -206,18 +207,21 @@
         high[i] = jnp.full((1, rows), -1e30, jnp.float32)
         total[i] = jnp.zeros((1, rows), jnp.float32)
 
-    def attend(src, g, sides, seen):
+    def attend(src, g, sides, seen, cols=slice(None)):
         keys = kv[src, g, 0 if seen else k_at : f_at, :]
         values = kv[src, g, v_at : n_at + fresh if seen else n_at, :].T
         key_frame = kv[src, g, f_at:v_at, :].astype(jnp.float32)[0:1, 0:1]
         key_position = iota((fresh, 1), 0) + (2 * src + side) * fresh
         new_frame = frame_of(key_position)
-        slope = slope_rows[g]
-        before = [(high[2 * g + r], total[2 * g + r], acc[2 * g + r]) for r in sides]
+        slope = slope_rows[g, :, cols]
+        before = [
+            (high[2 * g + r, :, cols], total[2 * g + r, :, cols], acc[2 * g + r, :, cols])
+            for r in sides
+        ]
         after = []
         for r, (top, sums, out) in zip(sides, before):
-            score = nt(keys, qb[r, g]) * scale
-            here = query_position(r)
+            score = nt(keys, qb[r, g, cols]) * scale
+            here = query_position(r)[:, cols]
             shift = slope * (key_frame - frame_of(here))
             old = score[fresh:] if seen else score
             now = jnp.maximum(top, jnp.max(old, axis=0, keepdims=True) + shift)
@@ -236,9 +240,9 @@
             out = out * corr + jnp.dot(values, weight, preferred_element_type=jnp.float32)
             after.append((now, sums * corr + fresh_sum, out))
         for r, (now, sums, out) in zip(sides, after):
-            high[2 * g + r] = now
-            total[2 * g + r] = sums
-            acc[2 * g + r] = out
+            high[2 * g + r, :, cols] = now
+            total[2 * g + r, :, cols] = sums
+            acc[2 * g + r, :, cols] = out
 
     def pass_on(apart, g):
         low = place - apart
@@ -262,17 +266,17 @@
                 def _():
                     slab_copy(top, g, h, False).start()
 
-    def attend_pair(apart, g, sides=(1, 0)):
+    def attend_pair(apart, g, sides=(1, 0), cols=slice(None)):
         low = place - apart
         top = place + apart
 
         @pl.when(low >= 0)
         def _():
-            attend(low, g, sides, True)
+            attend(low, g, sides, True, cols)
 
         @pl.when(top <= last)
         def _():
-            attend(top, g, sides, False)
+            attend(top, g, sides, False, cols)
 
     part_rows = rows // PARTS
     part_heads = group // PARTS
@@ -287,9 +291,9 @@
             device_id_type=MESH,
         )
 
-    def finish(g):
+    def finish(g, parts=range(PARTS)):
         sub = iota((16, part_rows), 0)
-        for c in range(PARTS):
+        for c in parts:
             i = g * PARTS + c
             cols = slice(c * part_rows, (c + 1) * part_rows)
             sums = total[2 * g + 1, :, cols]
@@ -375,8 +379,10 @@
     for c in range(PARTS):
         combine(c)
     pass_on(last, 1)
-    attend_pair(last, 1, (1,))
-    finish(1)
+    half = PARTS // 2
+    for c in (0, half):
+        attend_pair(last, 1, (1,), slice(c * part_rows, (c + half) * part_rows))
+        finish(1, range(c, c + half))
     attend_pair(last, 1, (0,))
     for c in range(PARTS):
         combine(count - PARTS + c)

time: 37.2 us -> 37.1 us (level)
  no operation moved by 1% of the time
where the time goes in v5:
time: 37.1 us; the launch traced here: 36.6 us
  Pallas kernels  34.9 us (94%)
  local copies, waits for them, and re-layouts  0.97 us (3%)
  between operations  0.66 us (2%)
    pallas_call x1, Pallas kernels, in_one_kernel(): pl.pallas_call(functools.partial(kernel, sizes), out_shape=pltpu.VMEM((fr...  34.9 us
    unnamed x1, local copies, waits for them, and re-layouts  0.97 us

profile of v5, /device:TPU:0, one launch (start us, length us, event | category | flops | bytes accessed | tf_op | source)
XLA Modules:
  0.0 36.6 jit_solution(17112320526589758989)
XLA Ops:
  0.7 34.9 %attend_over_slice.1 = bf16[64,8192]{1,0:T(8,128)(2,1)S(1)} custom-call(bf16[1024,128]{1,0:T(8,128)(2,1)} %bitcast.5, bf16[512,128]{1,0:T(8,128)(2,1)} %bitcast.6, bf16[512,128]{1,0:T(8,128)(2,1)} %bitcast.7, bf16[128,128]{1,0:T(8,128)(2,1)} %bitcast.8, bf16[128,128]{1,0:T(8,128)(2,1)} %bitcast.9, s32[1]{0:T(128)S(6)} %copy.10.frame_in, f32[16]{0:T(128)} %slope_in.1), custom_call_target="tpu_custom_call" | custom-call | tf_op jit(solution)/shard_map/attend_over_slice/pallas_call | solution.py:434
  35.6 1.0 %copy.9 = bf16[64,8192]{1,0:T(8,128)(2,1)} copy(bf16[64,8192]{1,0:T(8,128)(2,1)S(1)} %attend_over_slice.1) | data formatting | bytes 2097152

commit v6 on v5

--- a/solution.py
+++ b/solution.py
@@ -13,10 +13,6 @@
 MESH = pl.DeviceIdType.MESH
 LOG2E = 1.0 / math.log(2.0)
 PARTS = 4
-
-
-def nt(a, b):
-    return lax.dot_general(a, b, (((1,), (1,)), ((), ())), preferred_element_type=jnp.float32)
 
 
 def iota(shape, dim):
@@ -145,12 +141,16 @@
         for src, at, sel, n in (
             (nk_ref, 0, few, fresh),
             (ck_ref, k_at, pick, cached),
-            (cv_ref, v_at, pick, cached),
             (nv_ref, n_at, few, fresh),
         ):
             kv[place, g, at : at + n, :] = jnp.dot(
                 sel, src[...], preferred_element_type=jnp.float32
             ).astype(jnp.bfloat16)
+        turned = jnp.dot(pick, cv_ref[...], preferred_element_type=jnp.float32).T
+        for at in range(0, cached, width):
+            kv[place, g, v_at + at : v_at + at + width, :] = turned[:, at : at + width].astype(
+                jnp.bfloat16
+            )
         kv[place, g, f_at:v_at, :] = jnp.full((16, width), frame, jnp.float32).astype(jnp.bfloat16)
         if g == 0:
             pl.semaphore_wait(
@@ -183,7 +183,8 @@
             ],
             axis=0,
         )
-        qb[0, g] = jnp.dot(pick, q_ref[...], preferred_element_type=jnp.float32).astype(jnp.bfloat16)
+        ordered = jnp.dot(pick, q_ref[...], preferred_element_type=jnp.float32)
+        qb[0, g] = ordered.T.astype(jnp.bfloat16)
         q_copy(g).start()
 
     token = iota((1, rows), 1)
@@ -209,7 +210,10 @@
 
     def attend(src, g, sides, seen, cols=slice(None)):
         keys = kv[src, g, 0 if seen else k_at : f_at, :]
-        values = kv[src, g, v_at : n_at + fresh if seen else n_at, :].T
+        values = [kv[src, g, at : at + width, :] for at in range(v_at, n_at, width)]
+        if seen:
+            values.append(kv[src, g, n_at : n_at + fresh, :].T)
+        values = jnp.concatenate(values, axis=1)
         key_frame = kv[src, g, f_at:v_at, :].astype(jnp.float32)[0:1, 0:1]
         key_position = iota((fresh, 1), 0) + (2 * src + side) * fresh
         new_frame = frame_of(key_position)
@@ -220,7 +224,7 @@
         ]
         after = []
         for r, (top, sums, out) in zip(sides, before):
-            score = nt(keys, qb[r, g, cols]) * scale
+            score = jnp.dot(keys, qb[r, g, :, cols], preferred_element_type=jnp.float32) * scale
             here = query_position(r)[:, cols]
             shift = slope * (key_frame - frame_of(here))
             old = score[fresh:] if seen else score
@@ -445,7 +449,7 @@
             pltpu.SMEM(frame_of_slot.shape, jnp.int32),
             pltpu.SMEM(slopes.shape, jnp.float32),
             pltpu.VMEM((column, groups, slab, width), jnp.bfloat16),
-            pltpu.VMEM((2, groups, rows, width), jnp.bfloat16),
+            pltpu.VMEM((2, groups, width, rows), jnp.bfloat16),
             pltpu.VMEM((groups, 1, rows), jnp.float32),
             pltpu.VMEM((2 * groups, width, rows), jnp.float32),
             pltpu.VMEM((2 * groups, 1, rows), jnp.float32),
@@ -623,7 +627,7 @@
     cached = arrays[1].shape[0]
     frames = arrays[5].shape[0]
     shards, heads = lax.axis_size("ctx"), lax.axis_size("head")
-    whole_tiles = fresh % 16 == 0 and cached % 16 == 0 and width % 128 == 0
+    whole_tiles = fresh % 16 == 0 and cached % width == 0 and width % 128 == 0
     pairs = shards % 2 == 0 and shards > 6 and heads % 2 == 0 and arrays[1].shape[1] == 2
     if whole_tiles and pairs and frames == 1 and (local // arrays[1].shape[1]) % PARTS == 0:
         return in_one_kernel(*arrays)

time: 37.1 us -> 37.1 us (level)
  no operation moved by 1% of the time
where the time goes in v6:
time: 37.1 us; the launch traced here: 36.6 us
  Pallas kernels  34.9 us (94%)
  local copies, waits for them, and re-layouts  0.97 us (3%)
  between operations  0.66 us (2%)
    pallas_call x1, Pallas kernels, in_one_kernel(): pl.pallas_call(functools.partial(kernel, sizes), out_shape=pltpu.VMEM((fr...  34.9 us
    unnamed x1, local copies, waits for them, and re-layouts  0.97 us

profile of v6, /device:TPU:0, one launch (start us, length us, event | category | flops | bytes accessed | tf_op | source)
XLA Modules:
  0.0 36.6 jit_solution(580815806137359922)
XLA Ops:
  0.7 34.9 %attend_over_slice.1 = bf16[64,8192]{1,0:T(8,128)(2,1)S(1)} custom-call(bf16[1024,128]{1,0:T(8,128)(2,1)} %bitcast.5, bf16[512,128]{1,0:T(8,128)(2,1)} %bitcast.6, bf16[512,128]{1,0:T(8,128)(2,1)} %bitcast.7, bf16[128,128]{1,0:T(8,128)(2,1)} %bitcast.8, bf16[128,128]{1,0:T(8,128)(2,1)} %bitcast.9, s32[1]{0:T(128)S(6)} %copy.10.frame_in, f32[16]{0:T(128)} %slope_in.1), custom_call_target="tpu_custom_call" | custom-call | tf_op jit(solution)/shard_map/attend_over_slice/pallas_call | solution.py:438
  35.6 1.0 %copy.9 = bf16[64,8192]{1,0:T(8,128)(2,1)} copy(bf16[64,8192]{1,0:T(8,128)(2,1)S(1)} %attend_over_slice.1) | data formatting | bytes 2097152

commit v7 on v6

--- a/solution.py
+++ b/solution.py
@@ -81,9 +81,9 @@
             (
                 (ck_in, ck_ref),
                 (nk_in, nk_ref),
+                (frame_in, frame_ref),
                 (cv_in, cv_ref),
                 (nv_in, nv_ref),
-                (frame_in, frame_ref),
                 (q_in, q_ref),
                 (slope_in, slope_ref),
             )
@@ -132,7 +132,7 @@
 
     slant = iota((cached, groups * cached), 1) - groups * iota((cached, groups * cached), 0)
     picks = [(slant == g).astype(jnp.float32).astype(jnp.bfloat16) for g in range(groups)]
-    for fetch in fetches[:5]:
+    for fetch in fetches[:3]:
         fetch.wait()
     frame = frame_ref[0].astype(jnp.float32)
     for g in range(groups):
@@ -141,23 +141,28 @@
         for src, at, sel, n in (
             (nk_ref, 0, few, fresh),
             (ck_ref, k_at, pick, cached),
-            (nv_ref, n_at, few, fresh),
         ):
             kv[place, g, at : at + n, :] = jnp.dot(
                 sel, src[...], preferred_element_type=jnp.float32
             ).astype(jnp.bfloat16)
+        kv[place, g, f_at:v_at, :] = jnp.full((16, width), frame, jnp.float32).astype(jnp.bfloat16)
+        if g == 0:
+            pl.semaphore_wait(
+                barrier, 1 + heads // 2 + jnp.minimum(place, 1) + jnp.minimum(last - place, 1)
+            )
+
+        send_own(g, 0)
+        if g == 0:
+            for fetch in fetches[3:5]:
+                fetch.wait()
         turned = jnp.dot(pick, cv_ref[...], preferred_element_type=jnp.float32).T
         for at in range(0, cached, width):
             kv[place, g, v_at + at : v_at + at + width, :] = turned[:, at : at + width].astype(
                 jnp.bfloat16
             )
-        kv[place, g, f_at:v_at, :] = jnp.full((16, width), frame, jnp.float32).astype(jnp.bfloat16)
-        if g == 0:
-            pl.semaphore_wait(
-                barrier, 1 + heads // 2 + jnp.minimum(place, 1) + jnp.minimum(last - place, 1)
-            )
-
-        send_own(g, 0)
+        kv[place, g, n_at : n_at + fresh, :] = jnp.dot(
+            few, nv_ref[...], preferred_element_type=jnp.float32
+        ).astype(jnp.bfloat16)
         if g == 0:
             send_own(g, 1)
 

time: 37.1 us -> 37.1 us (level)
  no operation moved by 1% of the time
where the time goes in v7:
time: 37.1 us; the launch traced here: 36.6 us
  Pallas kernels  34.9 us (94%)
  local copies, waits for them, and re-layouts  0.97 us (3%)
  between operations  0.66 us (2%)
    pallas_call x1, Pallas kernels, in_one_kernel(): pl.pallas_call(functools.partial(kernel, sizes), out_shape=pltpu.VMEM((fr...  34.9 us
    unnamed x1, local copies, waits for them, and re-layouts  0.97 us

profile of v7, /device:TPU:0, one launch (start us, length us, event | category | flops | bytes accessed | tf_op | source)
XLA Modules:
  0.0 36.6 jit_solution(14025573755425015899)
XLA Ops:
  0.7 34.9 %attend_over_slice.1 = bf16[64,8192]{1,0:T(8,128)(2,1)S(1)} custom-call(bf16[1024,128]{1,0:T(8,128)(2,1)} %bitcast.5, bf16[512,128]{1,0:T(8,128)(2,1)} %bitcast.6, bf16[512,128]{1,0:T(8,128)(2,1)} %bitcast.7, bf16[128,128]{1,0:T(8,128)(2,1)} %bitcast.8, bf16[128,128]{1,0:T(8,128)(2,1)} %bitcast.9, s32[1]{0:T(128)S(6)} %copy.10.frame_in, f32[16]{0:T(128)} %slope_in.1), custom_call_target="tpu_custom_call" | custom-call | tf_op jit(solution)/shard_map/attend_over_slice/pallas_call | solution.py:443
  35.6 1.0 %copy.9 = bf16[64,8192]{1,0:T(8,128)(2,1)} copy(bf16[64,8192]{1,0:T(8,128)(2,1)S(1)} %attend_over_slice.1) | data formatting | bytes 2097152
